TPU v7x, 128 devices: a whole 4x4x4 slice. The times are simulated.
128 devices in a mesh: blk: 16 (over z, y_lo, core), grp: 8 (over x, y_hi).
Axes of the slice: x: 4, y: 4 (y_hi: 2, y_lo: 2; y = y_hi * 2 + y_lo), z: 4, core: 2. Of those that a mesh axis runs over, the one named last changes fastest.
Arguments:
- tgt_pos: float32 [3, 524288], P(None, ('blk', 'grp')), may hold values from -6 to 6
- tgt_area: float32 [524288], P(('blk', 'grp')), may hold values from 0.5 to 2
- tgt_cond: int32 [524288], P(('blk', 'grp')), may hold values from 0 to 63
- adjoint: float32 [64, 524288], P(None, ('blk', 'grp')), may hold values from -6 to 6
- src_pos: float32 [3, 8192], P(None, 'blk'), may hold values from -6 to 6
- src_nrm: float32 [3, 8192], P(None, 'blk'), may hold values from -6 to 6
- src_area: float32 [8192], P('blk'), may hold values from 0.005 to 0.05
- density: float32 [64, 8192], P(None, 'blk'), may hold values from -6 to 6
- cond_scale: float32 [64], replicated, may hold values from 0.5 to 4
- near_tgt: int32 [524288], P(('blk', 'grp')), may hold values from 0 to 524287, as said below
- near_src: int32 [524288], P(('blk', 'grp')), may hold values from 0 to 8191
- near_coef: float32 [524288], P(('blk', 'grp')), may hold values from 0.02 to 0.2
Outputs:
- tgt_grad: float32 [3, 524288], P(None, ('blk', 'grp'))
- src_grad: float32 [3, 8192], P(None, ('blk', 'grp'))
Inputs may be any that keep to these rules, and one draw needn't show every extreme that they name: Entry p of near_tgt lies among the targets k * 4096 to (k + 1) * 4096 - 1 with k = p // 4096.
All inputs are finite; a program needn't handle non-finite values.
Results may differ from a plain program's by a relative error of at most 0.0003.
Values sent between devices are 32-bit elements; how exact they have to be, the bound alone decides.
A program may use at most 768 MiB of HBM per device.

v0:
```python
import math

import jax
import jax.numpy as jnp
from jax import lax
from jax.sharding import PartitionSpec as P

SOFTEN = 0.05
INV_FOUR_PI = 1.0 / (4.0 * math.pi)
HIGH = lax.Precision.HIGHEST


def shifted(x, axis, by):
    devices = lax.axis_size(axis)
    return lax.ppermute(x, axis, [(i, (i + by) % devices) for i in range(devices)])


def block_terms(targets, packed):
    tgt_pos, weight_t, adjoint = targets
    width = adjoint.shape[0]
    density = packed[:width]
    src_pos = packed[width : width + 3]
    src_nrm = packed[width + 3 : width + 6]
    src_area = packed[width + 6]
    coupling = lax.dot_general(adjoint, density, (((0,), (0,)), ((), ())), precision=HIGH)
    scale = weight_t[:, None] * src_area[None, :] * coupling * INV_FOUR_PI
    dx = tgt_pos[0][:, None] - src_pos[0][None, :]
    dy = tgt_pos[1][:, None] - src_pos[1][None, :]
    dz = tgt_pos[2][:, None] - src_pos[2][None, :]
    r2 = dx * dx + dy * dy + dz * dz + SOFTEN
    inv = lax.rsqrt(r2)
    inv3 = inv * inv * inv
    ndot = src_nrm[0][None, :] * dx + src_nrm[1][None, :] * dy + src_nrm[2][None, :] * dz
    radial = 3.0 * ndot * inv3 * inv * inv
    gx = (src_nrm[0][None, :] * inv3 - radial * dx) * scale
    gy = (src_nrm[1][None, :] * inv3 - radial * dy) * scale
    gz = (src_nrm[2][None, :] * inv3 - radial * dz) * scale
    grad_t = jnp.stack([jnp.sum(gx, 1), jnp.sum(gy, 1), jnp.sum(gz, 1)])
    grad_s = -jnp.stack([jnp.sum(gx, 0), jnp.sum(gy, 0), jnp.sum(gz, 0)])
    return (grad_t, grad_s)


def per_device(
    tgt_pos,
    tgt_area,
    tgt_cond,
    adjoint,
    src_pos,
    src_nrm,
    src_area,
    density,
    cond_scale,
    near_tgt,
    near_src,
    near_coef,
):
    blocks = lax.axis_size("blk")
    width = adjoint.shape[0]
    tgt_count = tgt_pos.shape[1]
    src_count = src_pos.shape[1]
    total = src_count * blocks
    me_blk = lax.axis_index("blk")
    device = me_blk * lax.axis_size("grp") + lax.axis_index("grp")
    cond_hit = (tgt_cond[None, :] == lax.iota(jnp.int32, width)[:, None]).astype(jnp.float32)
    weight_t = tgt_area * jnp.sum(cond_hit * cond_scale[:, None], axis=0)
    local_pair = jnp.clip(near_tgt - device * tgt_count, 0, tgt_count - 1)
    pair_adj = jnp.take(adjoint, local_pair, axis=1)
    pair_weight = near_coef * jnp.take(weight_t, local_pair, axis=0)
    targets = (tgt_pos, weight_t, adjoint)
    source_pack = jnp.concatenate([density, src_pos, src_nrm, src_area[None, :]], axis=0)
    zeros_t = jnp.zeros((3, tgt_count), jnp.float32)
    start_home = me_blk * src_count
    moving = jnp.concatenate([source_pack, jnp.zeros((3, src_count), jnp.float32)], axis=0)

    def visit(step, carry):
        grad_t, held = carry
        part_t, part_s = block_terms(targets, held[: width + 7])
        held = held.at[width + 7 :].add(part_s)
        held = shifted(held, "blk", 1)
        return (grad_t + part_t, held)

    tgt_grad, moving = lax.fori_loop(0, blocks, visit, (zeros_t, moving))
    partial_value = lax.dynamic_update_slice_in_dim(
        jnp.zeros((3, total), jnp.float32), moving[width + 7 :], start_home, 1
    )
    near_pack = lax.all_gather(
        jnp.concatenate([density, src_nrm], axis=0), "blk", axis=1, tiled=True
    )
    picked = jnp.take(near_pack, near_src, axis=1)
    coupled = jnp.sum(pair_adj * picked[:width], axis=0) * pair_weight
    pair_val = coupled[None, :] * picked[width:]
    partial_value = partial_value.at[:, near_src].add(-pair_val)
    src_grad = lax.psum_scatter(partial_value, ("blk", "grp"), scatter_dimension=1, tiled=True)
    tgt_grad = tgt_grad.at[:, local_pair].add(pair_val)
    return (tgt_grad, src_grad)


def solution(mesh):
    placed = (
        P(None, ("blk", "grp")),
        P(("blk", "grp")),
        P(("blk", "grp")),
        P(None, ("blk", "grp")),
        P(None, "blk"),
        P(None, "blk"),
        P("blk"),
        P(None, "blk"),
        P(),
        P(("blk", "grp")),
        P(("blk", "grp")),
        P(("blk", "grp")),
    )
    return jax.shard_map(
        per_device,
        mesh=mesh,
        in_specs=placed,
        out_specs=(P(None, ("blk", "grp")), P(None, ("blk", "grp"))),
        check_vma=False,
    )
```

profile of v0, /device:TPU:1, one launch (start us, length us, event | category | flops | bytes accessed | tf_op | source)
XLA Modules:
  0.0 1194.0 jit_solution(7252335649862650243)
XLA Ops:
  10.0 1.8 copy.28
  15.5 14.1 %gather_fusion = f32[4096,64]{1,0:T(8,128)} fusion(f32[64,4096]{0,1:T(8,128)S(1)} %copy.28, s32[4096]{0:T(1024)S(1)} %broadcast_clamp_fusion.1), kind=kCustom, calls=%fused_computation | custom fusion | bytes 2113536 | tf_op jit(solution)/shard_map/jit(_take)/gather | solution.py:67
  29.6 40.5 %gather_fusion.2 = f32[4096]{0:T(1024)} fusion(f32[4096]{0:T(1024)S(1)} %mul.252, s32[4096]{0:T(1024)S(1)} %broadcast_clamp_fusion.1), kind=kCustom, calls=%fused_computation.2 | custom fusion | bytes 49152 | tf_op jit(solution)/shard_map/jit(_take)/gather | solution.py:68
  70.4 423.3 %while.16 = (s32[]{:T(128)}, f32[3,4096]{1,0:T(4,128)S(1)}, f32[74,512]{1,0:T(8,128)S(1)}, f32[3,4096]{1,0:T(4,128)S(1)}, f32[4096]{0:T(1024)S(1)}, /*index=5*/f...) while((s32[]{:T(128)}, f32[3,4096]{1,0:T(4,128)S(1)}, f32[74,512]{1,0:T(8,128)S(1)}, ...), condition=%wide.region_8.9_spmd.clone, body=%wide.region_1.8_spmd.clone.sunk | while | flops 1696637440 | bytes 52861072 | solution.py:82
  70.4 17.2 %fusion.40 = (f32[4096,512]{1,0:T(8,128)S(1)}, f32[4096,512]{1,0:T(8,128)S(1)}, f32[4096,512]{1,0:T(8,128)S(1)}) fusion(f32[512]{0:T(512)S(1)} %bitcast.77, f32[4096]{0:T(1024)S(1)} %bitcast.65, f32[512]{0:T(512)S(1)} %bitcast.75, f32[4096]{0:T(1024)S(1)} %bitcast.66, f32[512]{0:T(512)S(1)} %bitcast.76, f32[4096]{0:T(1024)S(1)} %bitcast.67, ...), kind=kOutput, calls=%fused_computation.25.clone.1 | convolution fusion | flops 1684013056 | bytes 26425344 | tf_op jit(solution)/shard_map/while/body/eval_jaxpr/dot_general | solution.py:25
  90.1 2.7 collective-permute-start
  92.9 2.2 collective-permute-done
  95.2 17.2 %fusion.40 = (f32[4096,512]{1,0:T(8,128)S(1)}, f32[4096,512]{1,0:T(8,128)S(1)}, f32[4096,512]{1,0:T(8,128)S(1)}) fusion(f32[512]{0:T(512)S(1)} %bitcast.77, f32[4096]{0:T(1024)S(1)} %bitcast.65, f32[512]{0:T(512)S(1)} %bitcast.75, f32[4096]{0:T(1024)S(1)} %bitcast.66, f32[512]{0:T(512)S(1)} %bitcast.76, f32[4096]{0:T(1024)S(1)} %bitcast.67, ...), kind=kOutput, calls=%fused_computation.25.clone.1 | convolution fusion | flops 1684013056 | bytes 26425344 | tf_op jit(solution)/shard_map/while/body/eval_jaxpr/dot_general | solution.py:25
  114.9 2.5 collective-permute-start
  117.5 2.4 collective-permute-done
  120.0 17.2 %fusion.40 = (f32[4096,512]{1,0:T(8,128)S(1)}, f32[4096,512]{1,0:T(8,128)S(1)}, f32[4096,512]{1,0:T(8,128)S(1)}) fusion(f32[512]{0:T(512)S(1)} %bitcast.77, f32[4096]{0:T(1024)S(1)} %bitcast.65, f32[512]{0:T(512)S(1)} %bitcast.75, f32[4096]{0:T(1024)S(1)} %bitcast.66, f32[512]{0:T(512)S(1)} %bitcast.76, f32[4096]{0:T(1024)S(1)} %bitcast.67, ...), kind=kOutput, calls=%fused_computation.25.clone.1 | convolution fusion | flops 1684013056 | bytes 26425344 | tf_op jit(solution)/shard_map/while/body/eval_jaxpr/dot_general | solution.py:25
  139.7 2.4 collective-permute-start
  142.1 4.5 collective-permute-done
  146.7 17.2 %fusion.40 = (f32[4096,512]{1,0:T(8,128)S(1)}, f32[4096,512]{1,0:T(8,128)S(1)}, f32[4096,512]{1,0:T(8,128)S(1)}) fusion(f32[512]{0:T(512)S(1)} %bitcast.77, f32[4096]{0:T(1024)S(1)} %bitcast.65, f32[512]{0:T(512)S(1)} %bitcast.75, f32[4096]{0:T(1024)S(1)} %bitcast.66, f32[512]{0:T(512)S(1)} %bitcast.76, f32[4096]{0:T(1024)S(1)} %bitcast.67, ...), kind=kOutput, calls=%fused_computation.25.clone.1 | convolution fusion | flops 1684013056 | bytes 26425344 | tf_op jit(solution)/shard_map/while/body/eval_jaxpr/dot_general | solution.py:25
  166.7 6.6 collective-permute-done
  173.4 17.2 %fusion.40 = (f32[4096,512]{1,0:T(8,128)S(1)}, f32[4096,512]{1,0:T(8,128)S(1)}, f32[4096,512]{1,0:T(8,128)S(1)}) fusion(f32[512]{0:T(512)S(1)} %bitcast.77, f32[4096]{0:T(1024)S(1)} %bitcast.65, f32[512]{0:T(512)S(1)} %bitcast.75, f32[4096]{0:T(1024)S(1)} %bitcast.66, f32[512]{0:T(512)S(1)} %bitcast.76, f32[4096]{0:T(1024)S(1)} %bitcast.67, ...), kind=kOutput, calls=%fused_computation.25.clone.1 | convolution fusion | flops 1684013056 | bytes 26425344 | tf_op jit(solution)/shard_map/while/body/eval_jaxpr/dot_general | solution.py:25
  193.2 6.7 collective-permute-done
  200.1 17.2 %fusion.40 = (f32[4096,512]{1,0:T(8,128)S(1)}, f32[4096,512]{1,0:T(8,128)S(1)}, f32[4096,512]{1,0:T(8,128)S(1)}) fusion(f32[512]{0:T(512)S(1)} %bitcast.77, f32[4096]{0:T(1024)S(1)} %bitcast.65, f32[512]{0:T(512)S(1)} %bitcast.75, f32[4096]{0:T(1024)S(1)} %bitcast.66, f32[512]{0:T(512)S(1)} %bitcast.76, f32[4096]{0:T(1024)S(1)} %bitcast.67, ...), kind=kOutput, calls=%fused_computation.25.clone.1 | convolution fusion | flops 1684013056 | bytes 26425344 | tf_op jit(solution)/shard_map/while/body/eval_jaxpr/dot_general | solution.py:25
  219.9 6.7 collective-permute-done
  226.7 17.2 %fusion.40 = (f32[4096,512]{1,0:T(8,128)S(1)}, f32[4096,512]{1,0:T(8,128)S(1)}, f32[4096,512]{1,0:T(8,128)S(1)}) fusion(f32[512]{0:T(512)S(1)} %bitcast.77, f32[4096]{0:T(1024)S(1)} %bitcast.65, f32[512]{0:T(512)S(1)} %bitcast.75, f32[4096]{0:T(1024)S(1)} %bitcast.66, f32[512]{0:T(512)S(1)} %bitcast.76, f32[4096]{0:T(1024)S(1)} %bitcast.67, ...), kind=kOutput, calls=%fused_computation.25.clone.1 | convolution fusion | flops 1684013056 | bytes 26425344 | tf_op jit(solution)/shard_map/while/body/eval_jaxpr/dot_general | solution.py:25
  246.6 6.7 collective-permute-done
  253.4 17.2 %fusion.40 = (f32[4096,512]{1,0:T(8,128)S(1)}, f32[4096,512]{1,0:T(8,128)S(1)}, f32[4096,512]{1,0:T(8,128)S(1)}) fusion(f32[512]{0:T(512)S(1)} %bitcast.77, f32[4096]{0:T(1024)S(1)} %bitcast.65, f32[512]{0:T(512)S(1)} %bitcast.75, f32[4096]{0:T(1024)S(1)} %bitcast.66, f32[512]{0:T(512)S(1)} %bitcast.76, f32[4096]{0:T(1024)S(1)} %bitcast.67, ...), kind=kOutput, calls=%fused_computation.25.clone.1 | convolution fusion | flops 1684013056 | bytes 26425344 | tf_op jit(solution)/shard_map/while/body/eval_jaxpr/dot_general | solution.py:25
  273.3 6.7 collective-permute-done
  280.1 17.2 %fusion.40 = (f32[4096,512]{1,0:T(8,128)S(1)}, f32[4096,512]{1,0:T(8,128)S(1)}, f32[4096,512]{1,0:T(8,128)S(1)}) fusion(f32[512]{0:T(512)S(1)} %bitcast.77, f32[4096]{0:T(1024)S(1)} %bitcast.65, f32[512]{0:T(512)S(1)} %bitcast.75, f32[4096]{0:T(1024)S(1)} %bitcast.66, f32[512]{0:T(512)S(1)} %bitcast.76, f32[4096]{0:T(1024)S(1)} %bitcast.67, ...), kind=kOutput, calls=%fused_computation.25.clone.1 | convolution fusion | flops 1684013056 | bytes 26425344 | tf_op jit(solution)/shard_map/while/body/eval_jaxpr/dot_general | solution.py:25
  300.0 6.7 collective-permute-done
  306.8 17.2 %fusion.40 = (f32[4096,512]{1,0:T(8,128)S(1)}, f32[4096,512]{1,0:T(8,128)S(1)}, f32[4096,512]{1,0:T(8,128)S(1)}) fusion(f32[512]{0:T(512)S(1)} %bitcast.77, f32[4096]{0:T(1024)S(1)} %bitcast.65, f32[512]{0:T(512)S(1)} %bitcast.75, f32[4096]{0:T(1024)S(1)} %bitcast.66, f32[512]{0:T(512)S(1)} %bitcast.76, f32[4096]{0:T(1024)S(1)} %bitcast.67, ...), kind=kOutput, calls=%fused_computation.25.clone.1 | convolution fusion | flops 1684013056 | bytes 26425344 | tf_op jit(solution)/shard_map/while/body/eval_jaxpr/dot_general | solution.py:25
  326.6 6.7 collective-permute-done
  333.5 17.2 %fusion.40 = (f32[4096,512]{1,0:T(8,128)S(1)}, f32[4096,512]{1,0:T(8,128)S(1)}, f32[4096,512]{1,0:T(8,128)S(1)}) fusion(f32[512]{0:T(512)S(1)} %bitcast.77, f32[4096]{0:T(1024)S(1)} %bitcast.65, f32[512]{0:T(512)S(1)} %bitcast.75, f32[4096]{0:T(1024)S(1)} %bitcast.66, f32[512]{0:T(512)S(1)} %bitcast.76, f32[4096]{0:T(1024)S(1)} %bitcast.67, ...), kind=kOutput, calls=%fused_computation.25.clone.1 | convolution fusion | flops 1684013056 | bytes 26425344 | tf_op jit(solution)/shard_map/while/body/eval_jaxpr/dot_general | solution.py:25
  353.3 6.7 collective-permute-done
  360.2 17.2 %fusion.40 = (f32[4096,512]{1,0:T(8,128)S(1)}, f32[4096,512]{1,0:T(8,128)S(1)}, f32[4096,512]{1,0:T(8,128)S(1)}) fusion(f32[512]{0:T(512)S(1)} %bitcast.77, f32[4096]{0:T(1024)S(1)} %bitcast.65, f32[512]{0:T(512)S(1)} %bitcast.75, f32[4096]{0:T(1024)S(1)} %bitcast.66, f32[512]{0:T(512)S(1)} %bitcast.76, f32[4096]{0:T(1024)S(1)} %bitcast.67, ...), kind=kOutput, calls=%fused_computation.25.clone.1 | convolution fusion | flops 1684013056 | bytes 26425344 | tf_op jit(solution)/shard_map/while/body/eval_jaxpr/dot_general | solution.py:25
  380.0 6.7 collective-permute-done
  386.9 17.2 %fusion.40 = (f32[4096,512]{1,0:T(8,128)S(1)}, f32[4096,512]{1,0:T(8,128)S(1)}, f32[4096,512]{1,0:T(8,128)S(1)}) fusion(f32[512]{0:T(512)S(1)} %bitcast.77, f32[4096]{0:T(1024)S(1)} %bitcast.65, f32[512]{0:T(512)S(1)} %bitcast.75, f32[4096]{0:T(1024)S(1)} %bitcast.66, f32[512]{0:T(512)S(1)} %bitcast.76, f32[4096]{0:T(1024)S(1)} %bitcast.67, ...), kind=kOutput, calls=%fused_computation.25.clone.1 | convolution fusion | flops 1684013056 | bytes 26425344 | tf_op jit(solution)/shard_map/while/body/eval_jaxpr/dot_general | solution.py:25
  406.7 6.7 collective-permute-done
  413.5 17.2 %fusion.40 = (f32[4096,512]{1,0:T(8,128)S(1)}, f32[4096,512]{1,0:T(8,128)S(1)}, f32[4096,512]{1,0:T(8,128)S(1)}) fusion(f32[512]{0:T(512)S(1)} %bitcast.77, f32[4096]{0:T(1024)S(1)} %bitcast.65, f32[512]{0:T(512)S(1)} %bitcast.75, f32[4096]{0:T(1024)S(1)} %bitcast.66, f32[512]{0:T(512)S(1)} %bitcast.76, f32[4096]{0:T(1024)S(1)} %bitcast.67, ...), kind=kOutput, calls=%fused_computation.25.clone.1 | convolution fusion | flops 1684013056 | bytes 26425344 | tf_op jit(solution)/shard_map/while/body/eval_jaxpr/dot_general | solution.py:25
  433.4 6.7 collective-permute-done
  440.2 17.2 %fusion.40 = (f32[4096,512]{1,0:T(8,128)S(1)}, f32[4096,512]{1,0:T(8,128)S(1)}, f32[4096,512]{1,0:T(8,128)S(1)}) fusion(f32[512]{0:T(512)S(1)} %bitcast.77, f32[4096]{0:T(1024)S(1)} %bitcast.65, f32[512]{0:T(512)S(1)} %bitcast.75, f32[4096]{0:T(1024)S(1)} %bitcast.66, f32[512]{0:T(512)S(1)} %bitcast.76, f32[4096]{0:T(1024)S(1)} %bitcast.67, ...), kind=kOutput, calls=%fused_computation.25.clone.1 | convolution fusion | flops 1684013056 | bytes 26425344 | tf_op jit(solution)/shard_map/while/body/eval_jaxpr/dot_general | solution.py:25
  460.1 6.7 collective-permute-done
  466.9 17.2 %fusion.40 = (f32[4096,512]{1,0:T(8,128)S(1)}, f32[4096,512]{1,0:T(8,128)S(1)}, f32[4096,512]{1,0:T(8,128)S(1)}) fusion(f32[512]{0:T(512)S(1)} %bitcast.77, f32[4096]{0:T(1024)S(1)} %bitcast.65, f32[512]{0:T(512)S(1)} %bitcast.75, f32[4096]{0:T(1024)S(1)} %bitcast.66, f32[512]{0:T(512)S(1)} %bitcast.76, f32[4096]{0:T(1024)S(1)} %bitcast.67, ...), kind=kOutput, calls=%fused_computation.25.clone.1 | convolution fusion | flops 1684013056 | bytes 26425344 | tf_op jit(solution)/shard_map/while/body/eval_jaxpr/dot_general | solution.py:25
  486.8 6.7 collective-permute-done
  493.9 2.2 broadcast_in_dim.59
  496.9 16.3 %gather_fusion.1 = f32[4096,67]{1,0:T(8,128)} fusion(f32[67,8192]{0,1:T(8,128)} %all-gather.2.cloned.1.call-done, s32[4096]{0:T(1024)S(1)} %get-tuple-element.158), kind=kCustom, calls=%fused_computation.1 | custom fusion | bytes 2211840 | tf_op jit(solution)/shard_map/jit(_take)/gather | solution.py:89
  513.2 3.6 select_bitcast_fusion
  516.8 2.5 fusion.16
  519.4 26.3 %scatter_custom_fusion.1 = f32[3,8192]{0,1:T(8,128)} fusion(f32[3,8192]{0,1:T(8,128)} %constant_dynamic-update-slice_fusion, s32[4096]{0:T(1024)S(1)} %get-tuple-element.157, f32[67,4096]{0,1:T(8,128)S(1)} %select_bitcast_fusion, f32[4096]{0:T(1024)S(1)} %multiply_multiply_fusion.3), kind=kCustom, calls=%fused_computation.38 | custom fusion | flops 36864 | bytes 2211840 | tf_op jit(solution)/shard_map/scatter-add | solution.py:92
  545.7 2.0 copy.31
  547.7 25.2 %scatter_custom_fusion = f32[3,4096]{0,1:T(8,128)} fusion(f32[3,4096]{0,1:T(8,128)} %copy.31, s32[4096]{0:T(1024)} %copy-done.4, f32[67,4096]{0,1:T(8,128)S(1)} %select_bitcast_fusion, f32[4096]{0:T(1024)S(1)} %multiply_multiply_fusion.3), kind=kCustom, calls=%fused_computation.40 | custom fusion | flops 24576 | bytes 1163264 | tf_op jit(solution)/shard_map/scatter-add | solution.py:94
  572.8 2.8 copy.33
  575.7 610.1 %reduce-scatter.2.cloned.1.call-done = f32[3,64]{0,1:T(8,128)} async-done(((f32[3,8192]{0,1:T(8,128)}), f32[3,64]{0,1:T(8,128)}) %reduce-scatter.2.cloned.1.call-update) | async-done | bytes 784 | tf_op jit(solution)/shard_map/reduce_scatter | solution.py:93
  (185 shorter events, 51.7 us)
Async XLA Ops:
  7.2 489.7 %all-gather.2.cloned.1.call-start = ((), (), s32[]{:S(2)}) async-start(), calls=%async_computation.1 | async-start | bytes 4456448 | tf_op jit(solution)/shard_map/all_gather | solution.py:86
  10.0 1175.7 %reduce-scatter.2.cloned.1.call-start = ((), (), s32[]{:S(2)}) async-start(), calls=%async_computation.2 | async-start | bytes 4227072 | tf_op jit(solution)/shard_map/reduce_scatter | solution.py:93
  13.2 0.6 copy-start.4
  29.6 40.6 %copy-start.2 = (f32[64,512]{1,0:T(8,128)S(1)}, f32[64,512]{1,0:T(8,128)}, u32[]{:S(2)}) copy-start(f32[64,512]{1,0:T(8,128)} %param.23) | copy-start | bytes 393220
  29.6 40.6 %copy-start.7 = (f32[3,512]{1,0:T(4,128)S(1)}, f32[3,512]{1,0:T(4,128)}, u32[]{:S(2)}) copy-start(f32[3,512]{1,0:T(4,128)} %param.21) | copy-start | bytes 18436
  29.6 40.6 %copy-start.9 = (f32[3,512]{1,0:T(4,128)S(1)}, f32[3,512]{1,0:T(4,128)}, u32[]{:S(2)}) copy-start(f32[3,512]{1,0:T(4,128)} %param.20) | copy-start | bytes 18436
  29.6 40.6 %copy-start.10 = (f32[512]{0:T(512)S(1)}, f32[512]{0:T(512)}, u32[]{:S(2)}) copy-start(f32[512]{0:T(512)} %param.22) | copy-start | bytes 6148
  29.6 40.7 %copy-start = (f32[64,4096]{1,0:T(8,128)S(1)}, f32[64,4096]{1,0:T(8,128)}, u32[]{:S(2)}) copy-start(f32[64,4096]{1,0:T(8,128)} %param.19) | copy-start | bytes 3145732
  29.6 40.7 %copy-start.1 = (f32[3,4096]{1,0:T(4,128)S(1)}, f32[3,4096]{1,0:T(4,128)}, u32[]{:S(2)}) copy-start(f32[3,4096]{1,0:T(4,128)} %param.16) | copy-start | bytes 147460
  70.3 426.5 %copy-start.3 = (s32[4096]{0:T(1024)S(1)}, s32[4096]{0:T(1024)}, u32[]{:S(2)}) copy-start(s32[4096]{0:T(1024)} %param.26) | copy-start | bytes 49156
  90.1 5.0 collective-permute-start
  114.9 5.0 collective-permute-start
  139.7 6.9 collective-permute-start
  166.3 6.9 collective-permute-start
  193.0 6.9 collective-permute-start
  219.7 6.9 collective-permute-start
  246.4 6.9 collective-permute-start
  273.1 6.9 collective-permute-start
  299.8 6.9 collective-permute-start
  326.5 6.9 collective-permute-start
  353.2 6.9 collective-permute-start
  379.8 6.9 collective-permute-start
  406.5 6.9 collective-permute-start
  433.2 6.9 collective-permute-start
  459.9 6.9 collective-permute-start
  486.6 6.9 collective-permute-start
  496.1 20.7 %copy-start.6 = (pred[4096]{0:T(1024)(128)(4,1)S(1)}, pred[4096]{0:T(1024)(128)(4,1)}, u32[]{:S(2)}) copy-start(pred[4096]{0:T(1024)(128)(4,1)} %get-tuple-element.140) | copy-start | bytes 12292
  496.9 22.4 %copy-start.5 = (f32[4096]{0:T(1024)S(1)}, f32[4096]{0:T(1024)}, u32[]{:S(2)}) copy-start(f32[4096]{0:T(1024)} %gather_fusion.2) | copy-start | bytes 49156
  496.9 22.4 %copy-start.8 = (f32[4096]{0:T(1024)S(1)}, f32[4096]{0:T(1024)}, u32[]{:S(2)}) copy-start(f32[4096]{0:T(1024)} %param.27) | copy-start | bytes 49156
Sparse Core Ops, SparseCore 0:
  10.1 41.0 all-gather.1
  545.8 639.8 reduce-scatter.1
where the time goes:
time: 1200 us; the launch traced here: 1190 us
  waiting for transfers between devices  707 us (59%)
  matrix products  275 us (23%)
  other arithmetic  98.9 us (8%)
  local copies, waits for them, and re-layouts  88.9 us (7%)
  between operations  14.3 us (1%)
    reduce_scatter x1, waiting for transfers between devices, per_device(): lax.psum_scatter(partial_value, ('blk', 'grp'), scatter_dimension=1, tile...  610 us
    dot_general x16, matrix products, block_terms(): lax.dot_general(adjoint, density, (((0,), (0,)), ((), ())), precision=HIGH)  275 us
    ppermute x16, waiting for transfers between devices, shifted(): lax.ppermute(x, axis, [(i, (i + by) % devices) for i in range(devices)])  96.5 us
    gather x1, local copies, waits for them, and re-layouts, per_device(): pair_weight = near_coef * jnp.take(weight_t, local_pair, axis=0)  40.5 us
    reduce_sum x32, other arithmetic, block_terms(): grad_s = -jnp.stack([jnp.sum(gx, 0), jnp.sum(gy, 0), jnp.sum(gz, 0)])  35.7 us
    scatter-add x1, other arithmetic, per_device(): partial_value = partial_value.at[:, near_src].add(-pair_val)  26.3 us
    scatter-add x1, other arithmetic, per_device(): tgt_grad = tgt_grad.at[:, local_pair].add(pair_val)  25.2 us
  transfers between devices with their start and end apart: 18, of which 17 were waited for; matrix products, arithmetic and copies ran while one was open for 34% of the time, Pallas kernels for 0%

commit v1 on v0

v1 whole, which is shorter than its diff:
```python
import functools
import math

import jax
import jax.numpy as jnp
from jax import lax
from jax.experimental import pallas as pl
from jax.experimental.pallas import tpu as pltpu
from jax.sharding import PartitionSpec as P

SOFTEN = 0.05
INV_FOUR_PI = 1.0 / (4.0 * math.pi)
MESH = pl.DeviceIdType.MESH
F32 = jnp.float32
BF16 = jnp.bfloat16
LANES = 128
WIDTH = 64
PACK = 72
BLOCK = 256
CHUNK = 512
SUM_ROWS = 16


def part(x):
    return x.astype(BF16).astype(F32)


def three_parts(x):
    first = part(x)
    second = part(x - first)
    return first, second, part(x - first - second)


def grid_parts(x):
    first = jnp.floor(x * 16.0 + 0.5) * 0.0625
    rest = x - first
    second = part(rest)
    return first, second, part(rest - second), rest


def square_parts(first, rest):
    square = jnp.sum(first * first, axis=0, keepdims=True)
    whole = jnp.floor(square)
    left = jnp.sum((2.0 * first + rest) * rest, axis=0, keepdims=True)
    return whole, square - whole, left


def rows(pieces, total):
    count = sum(p.shape[0] for p in pieces)
    width = pieces[0].shape[1]
    if count < total:
        pieces = list(pieces) + [jnp.zeros((total - count, width), F32)]
    return jnp.concatenate(pieces, axis=0)


def target_features(pos):
    t1, t2, t3, rest = grid_parts(pos)
    whole, fraction, left = square_parts(t1, rest)
    ones = jnp.ones((5, pos.shape[1]), F32)
    return rows([ones, t1, whole, fraction, t1, t1, t2, t2, t2, t3, t3, *three_parts(left)], WIDTH)


def source_features(pos, nrm):
    s1, s2, s3, rest = grid_parts(pos)
    whole, fraction, left = square_parts(s1, rest)
    zero = jnp.zeros((1, pos.shape[1]), F32)
    one = jnp.ones((1, pos.shape[1]), F32)
    radius = rows(
        [whole, fraction, *three_parts(left + SOFTEN)]
        + [-2.0 * s1, one, one, -2.0 * s2, -2.0 * s3, -2.0 * s1, -2.0 * s2, -2.0 * s3, -2.0 * s1, -2.0 * s2]
        + [one, one, one],
        WIDTH,
    )
    triple = 3.0 * nrm
    n1, n2, n3 = three_parts(triple)
    offset = -jnp.sum(triple * pos, axis=0, keepdims=True)
    normal = rows(
        [*three_parts(offset), zero, zero]
        + [n1, zero, zero, n2, n3, n1, n2, n3, n1, n2]
        + [zero, zero, zero],
        WIDTH,
    )
    return radius, normal


def pair_kernel(
    near_tgt, near_src, tgt_pos, tgt_area, tgt_cond, adjoint, cond_scale, near_tgt_row, near_src_row, near_coef, packs,
    tgt_out, src_out,
    held, left_m, rhs_c, rhs_g, src_rows, src_table, spread, tgt_sum, src_sum, product, buf0, buf1,
):
    tgt_count = tgt_pos.shape[1]
    parts, _, per = packs.shape
    total = parts * per
    halves = per // BLOCK
    blocks = total // BLOCK
    chunks = tgt_count // CHUNK

    def target_prep(i, _):
        cols = pl.ds(pl.multiple_of(i * CHUNK, CHUNK), CHUNK)
        cond = tgt_cond[:, cols]
        hit = lax.broadcasted_iota(jnp.int32, (WIDTH, CHUNK), 0) == cond
        weight = tgt_area[:, cols] * jnp.sum(jnp.where(hit, cond_scale[...], 0.0), axis=0, keepdims=True)
        stacked = jnp.concatenate([adjoint[:, cols] * weight, target_features(tgt_pos[:, cols])], axis=0)
        flat = jnp.transpose(stacked)
        held[cols, :] = flat
        high = part(flat)
        low = flat - high
        lane = lax.broadcasted_iota(jnp.int32, (CHUNK, LANES), 1)
        second = jnp.where(lane >= WIDTH, pltpu.roll(high, WIDTH, 1), low)
        left_m[cols, 0:LANES] = high.astype(BF16)
        left_m[cols, LANES : 2 * LANES] = second.astype(BF16)
        return 0

    lax.fori_loop(0, chunks, target_prep, 0)

    feature = lax.broadcasted_iota(jnp.int32, (LANES, 3 * LANES), 0) - WIDTH
    which = lax.broadcasted_iota(jnp.int32, (LANES, 3 * LANES), 1) // LANES
    pick = (feature == 5 + which) | (feature == 16 + which) | (feature == 25 + which)
    picker = pick.astype(F32).astype(BF16)

    def spread_prep(i, _):
        cols = pl.ds(pl.multiple_of(i * CHUNK, CHUNK), CHUNK)
        spread[cols, :] = jnp.dot(left_m[cols, 0:LANES], picker, preferred_element_type=F32)
        tgt_sum[cols, :] = jnp.zeros((CHUNK, 3 * LANES), F32)
        return 0

    lax.fori_loop(0, chunks, spread_prep, 0)

    zeros = jnp.zeros((WIDTH, BLOCK), BF16)

    def source_prep(b, _):
        for h in range(halves):
            pack = packs[b, :, h * BLOCK : (h + 1) * BLOCK]
            block = b * halves + h
            density = pack[0:WIDTH]
            pos = pack[WIDTH : WIDTH + 3]
            nrm = pack[WIDTH + 3 : WIDTH + 6]
            scaled = density * (pack[WIDTH + 6 : WIDTH + 7] * INV_FOUR_PI)
            high = scaled.astype(BF16)
            low = (scaled - high.astype(F32)).astype(BF16)
            rhs_c[block, 0:WIDTH, :] = high
            rhs_c[block, WIDTH : 2 * WIDTH, :] = zeros
            rhs_c[block, 2 * WIDTH : 3 * WIDTH, :] = high
            rhs_c[block, 3 * WIDTH : 4 * WIDTH, :] = low
            radius, normal = source_features(pos, nrm)
            rhs_g[block, 0:WIDTH, 0:BLOCK] = zeros
            rhs_g[block, 0:WIDTH, BLOCK : 2 * BLOCK] = zeros
            rhs_g[block, WIDTH : 2 * WIDTH, 0:BLOCK] = radius.astype(BF16)
            rhs_g[block, WIDTH : 2 * WIDTH, BLOCK : 2 * BLOCK] = normal.astype(BF16)
            src_rows[block] = pack[WIDTH : WIDTH + 8]
            src_sum[block] = jnp.zeros((24, BLOCK), F32)
            stacked = jnp.concatenate([density, rows([nrm], WIDTH)], axis=0)
            src_table[pl.ds(pl.multiple_of(block * BLOCK, BLOCK), BLOCK), :] = jnp.transpose(stacked)
        return 0

    lax.fori_loop(0, parts, source_prep, 0)

    steps = blocks * chunks

    def products(k, buf):
        b, i = k // chunks, lax.rem(k, chunks)
        rows_at = pl.ds(pl.multiple_of(i * CHUNK, CHUNK), CHUNK)
        buf[:, 0:BLOCK] = jnp.dot(left_m[rows_at, :], rhs_c[b], preferred_element_type=F32)
        buf[:, BLOCK : 3 * BLOCK] = jnp.dot(left_m[rows_at, 0:LANES], rhs_g[b], preferred_element_type=F32)

    def sums(k, buf):
        b, i = k // chunks, lax.rem(k, chunks)
        base = i * CHUNK
        src = src_rows[b]
        wide = BLOCK // LANES
        lane = [slice(j * LANES, (j + 1) * LANES) for j in range(wide)]
        row = [[jnp.broadcast_to(src[q : q + 1, lane[j]], (8, LANES)) for q in range(6)] for j in range(wide)]
        acc = [[src_sum[b, 8 * c : 8 * c + 8, lane[j]] for c in range(3)] for j in range(wide)]
        for r in range(CHUNK // 8):
            at = pl.ds(pl.multiple_of(base + 8 * r, 8), 8)
            here = [spread[at, c * LANES : (c + 1) * LANES] for c in range(3)]
            total_t = [None] * 3
            for j in range(wide):
                coupling = buf[8 * r : 8 * r + 8, j * LANES : (j + 1) * LANES]
                radius = buf[8 * r : 8 * r + 8, BLOCK + j * LANES : BLOCK + (j + 1) * LANES]
                normal = buf[8 * r : 8 * r + 8, 2 * BLOCK + j * LANES : 2 * BLOCK + (j + 1) * LANES]
                inv = lax.rsqrt(radius)
                inv2 = inv * inv
                scale = (coupling * inv) * inv2
                along = normal * inv2
                for c in range(3):
                    g = scale * (row[j][3 + c] - along * (here[c] - row[j][c]))
                    acc[j][c] = acc[j][c] + g
                    total_t[c] = g if total_t[c] is None else total_t[c] + g
            for c in range(3):
                tgt_sum[at, c * LANES : (c + 1) * LANES] += total_t[c]
        for j in range(wide):
            for c in range(3):
                src_sum[b, 8 * c : 8 * c + 8, lane[j]] = acc[j][c]

    products(0, buf0)

    def far(h, _):
        k = 2 * h
        products(k + 1, buf1)
        sums(k, buf0)
        products(jnp.minimum(k + 2, steps - 1), buf0)
        sums(k + 1, buf1)
        return 0

    lax.fori_loop(0, steps // 2, far, 0)

    pairs = near_coef.shape[1]
    first_target = (near_tgt[0] // tgt_count) * tgt_count

    def gather(i, _):
        for u in range(16):
            p = i * 16 + u
            t = near_tgt[p] - first_target
            product[pl.ds(p, 1), :] = held[pl.ds(t, 1), :] * src_table[pl.ds(near_src[p], 1), :]
        return 0

    lax.fori_loop(0, pairs // 16, gather, 0)

    flat = jnp.transpose(product[...])
    coupled = jnp.sum(flat[0:WIDTH], axis=0, keepdims=True) * near_coef[...]
    value = coupled * flat[WIDTH : WIDTH + 3]
    high = part(value)
    both = rows([high, part(value - high)], 8)

    def scatter(index, groups):
        row_at, lane_at = index // LANES, lax.rem(index, LANES)
        chosen = [jnp.where(row_at == g, both, 0.0).astype(BF16) for g in range(groups)]
        lanes = (lax.broadcasted_iota(jnp.int32, (LANES, pairs), 0) == lane_at).astype(F32).astype(BF16)
        return lax.dot_general(
            jnp.concatenate(chosen, axis=0), lanes, (((1,), (1,)), ((), ())), preferred_element_type=F32
        )

    local = near_tgt_row[...] - first_target
    to_tgt = scatter(local, tgt_count // LANES)
    to_src = scatter(near_src_row[...], total // LANES)

    lane = lax.broadcasted_iota(jnp.int32, (LANES, LANES), 1)
    for g in range(tgt_count // LANES):
        at = slice(g * LANES, (g + 1) * LANES)
        merged = jnp.zeros((LANES, LANES), F32)
        for c in range(3):
            one = jnp.sum(tgt_sum[at, c * LANES : (c + 1) * LANES], axis=1, keepdims=True)
            merged = jnp.where(lane == c, one, merged)
        near = to_tgt[8 * g : 8 * g + 8]
        tgt_out[:, at] = jnp.transpose(merged)[0:3] + near[0:3] + near[3:6]
    quarters = per // LANES
    for b in range(parts):
        src_out[b, 3 * quarters :, :] = jnp.zeros((src_out.shape[1] - 3 * quarters, LANES), F32)
        for q in range(quarters):
            g = b * quarters + q
            block, j = divmod(g, BLOCK // LANES)
            near = to_src[8 * g : 8 * g + 8]
            near = near[0:3] + near[3:6]
            at = slice(j * LANES, (j + 1) * LANES)
            for c in range(3):
                far_sum = jnp.sum(src_sum[block, 8 * c : 8 * c + 8, at], axis=0, keepdims=True)
                row = c * quarters + q
                src_out[b, row : row + 1, :] = -far_sum - near[c : c + 1]


def pair_sums(tgt_pos, tgt_area, tgt_cond, adjoint, cond_scale, near_tgt, near_src, near_coef, packs):
    tgt_count = tgt_pos.shape[1]
    pairs = near_coef.shape[0]
    parts, _, per = packs.shape
    total = parts * per
    blocks = total // BLOCK
    vmem = pl.BlockSpec(memory_space=pltpu.VMEM)
    smem = pl.BlockSpec(memory_space=pltpu.SMEM)
    return pl.pallas_call(
        pair_kernel,
        out_shape=[jax.ShapeDtypeStruct((3, tgt_count), F32), jax.ShapeDtypeStruct((parts, SUM_ROWS, LANES), F32)],
        in_specs=[smem, smem] + [vmem] * 9,
        out_specs=[vmem, vmem],
        scratch_shapes=[
            pltpu.VMEM((tgt_count, LANES), F32),
            pltpu.VMEM((tgt_count, 2 * LANES), BF16),
            pltpu.VMEM((blocks, 4 * WIDTH, BLOCK), BF16),
            pltpu.VMEM((blocks, 2 * WIDTH, 2 * BLOCK), BF16),
            pltpu.VMEM((blocks, 8, BLOCK), F32),
            pltpu.VMEM((total, LANES), F32),
            pltpu.VMEM((tgt_count, 3 * LANES), F32),
            pltpu.VMEM((tgt_count, 3 * LANES), F32),
            pltpu.VMEM((blocks, 24, BLOCK), F32),
            pltpu.VMEM((pairs, LANES), F32),
            pltpu.VMEM((CHUNK, 3 * BLOCK), F32),
            pltpu.VMEM((CHUNK, 3 * BLOCK), F32),
        ],
        compiler_params=pltpu.CompilerParams(vmem_limit_bytes=60 * 2**20),
    )(
        near_tgt, near_src, tgt_pos, tgt_area[None, :], tgt_cond[None, :], adjoint, cond_scale[:, None],
        near_tgt[None, :], near_src[None, :], near_coef[None, :], packs,
    )


def greet(peers):
    barrier = pltpu.get_barrier_semaphore()
    for peer in peers:
        pl.semaphore_signal(barrier, inc=1, device_id=peer, device_id_type=MESH)
    pl.semaphore_wait(barrier, len(peers))


def gather_kernel(n, own, out, send_sem, recv_sem, local_sem):
    me = lax.axis_index("blk")
    others = [lax.rem(me + k, n) for k in range(1, n)]
    greet([{"blk": other} for other in others])
    copies = []
    for k, other in enumerate(others):
        copy = pltpu.make_async_remote_copy(
            src_ref=own, dst_ref=out.at[me], send_sem=send_sem.at[k], recv_sem=recv_sem.at[k],
            device_id={"blk": other}, device_id_type=MESH,
        )
        copy.start()
        copies.append(copy)
    mine = pltpu.make_async_copy(own, out.at[me], local_sem)
    mine.start()
    mine.wait()
    for copy in copies:
        copy.wait()


def gather_sources(pack, n):
    hbm = pl.BlockSpec(memory_space=pl.ANY)
    return pl.pallas_call(
        functools.partial(gather_kernel, n),
        out_shape=jax.ShapeDtypeStruct((n,) + pack.shape, F32),
        in_specs=[hbm],
        out_specs=hbm,
        scratch_shapes=[
            pltpu.SemaphoreType.DMA((n - 1,)),
            pltpu.SemaphoreType.DMA((n - 1,)),
            pltpu.SemaphoreType.DMA,
        ],
        compiler_params=pltpu.CompilerParams(collective_id=0, has_side_effects=True),
    )(pack)


def reduce_kernel(n, groups, sums, out, first, second, mine, send1, recv1, send2, recv2):
    me, grp = lax.axis_index("blk"), lax.axis_index("grp")
    blk_others = [lax.rem(me + k, n) for k in range(1, n)]
    grp_others = [lax.rem(grp + k, groups) for k in range(1, groups)]
    greet([{"blk": other} for other in blk_others] + [{"grp": other} for other in grp_others])
    copies = []
    for k, other in enumerate(blk_others):
        copy = pltpu.make_async_remote_copy(
            src_ref=sums.at[other], dst_ref=first.at[k], send_sem=send1.at[k], recv_sem=recv1.at[k],
            device_id={"blk": other}, device_id_type=MESH,
        )
        copy.start()
        copies.append(copy)
    total = sums[me]
    for k, copy in enumerate(copies):
        copy.wait_recv()
        total = total + first[k]
    quarters = groups // 2
    for q in range(quarters):
        mine[q] = jnp.concatenate(
            [total[c * quarters + q : c * quarters + q + 1] for c in range(3)] + [jnp.zeros((5, LANES), F32)], axis=0
        )
    more = []
    for k, other in enumerate(grp_others):
        copy = pltpu.make_async_remote_copy(
            src_ref=mine.at[other // 2], dst_ref=second.at[k], send_sem=send2.at[k], recv_sem=recv2.at[k],
            device_id={"grp": other}, device_id_type=MESH,
        )
        copy.start()
        more.append(copy)
    result = mine[grp // 2]
    for k, copy in enumerate(more):
        copy.wait_recv()
        result = result + second[k]
    half = LANES // 2
    out[...] = jnp.where(lax.rem(grp, 2) == 1, result[0:3, half:], result[0:3, 0:half])
    for copy in copies + more:
        copy.wait_send()


def reduce_sources(sums, n, groups):
    vmem = pl.BlockSpec(memory_space=pltpu.VMEM)
    return pl.pallas_call(
        functools.partial(reduce_kernel, n, groups),
        out_shape=jax.ShapeDtypeStruct((3, LANES // 2), F32),
        in_specs=[vmem],
        out_specs=vmem,
        scratch_shapes=[
            pltpu.VMEM((n - 1, SUM_ROWS, LANES), F32),
            pltpu.VMEM((groups - 1, 8, LANES), F32),
            pltpu.VMEM((groups // 2, 8, LANES), F32),
            pltpu.SemaphoreType.DMA((n - 1,)),
            pltpu.SemaphoreType.DMA((n - 1,)),
            pltpu.SemaphoreType.DMA((groups - 1,)),
            pltpu.SemaphoreType.DMA((groups - 1,)),
        ],
        compiler_params=pltpu.CompilerParams(collective_id=1, has_side_effects=True),
    )(sums)


def per_device(
    tgt_pos, tgt_area, tgt_cond, adjoint, src_pos, src_nrm, src_area, density, cond_scale, near_tgt, near_src, near_coef
):
    n, groups = lax.axis_size("blk"), lax.axis_size("grp")
    filler = jnp.zeros((PACK - WIDTH - 7, src_pos.shape[1]), F32)
    pack = jnp.concatenate([density, src_pos, src_nrm, src_area[None, :], filler], axis=0)
    packs = gather_sources(pack, n)
    tgt_grad, sums = pair_sums(
        tgt_pos, tgt_area, tgt_cond, adjoint, cond_scale, near_tgt, near_src, near_coef, packs
    )
    return tgt_grad, reduce_sources(sums, n, groups)


def solution(mesh):
    placed = (
        P(None, ("blk", "grp")),
        P(("blk", "grp")),
        P(("blk", "grp")),
        P(None, ("blk", "grp")),
        P(None, "blk"),
        P(None, "blk"),
        P("blk"),
        P(None, "blk"),
        P(),
        P(("blk", "grp")),
        P(("blk", "grp")),
        P(("blk", "grp")),
    )
    return jax.shard_map(
        per_device,
        mesh=mesh,
        in_specs=placed,
        out_specs=(P(None, ("blk", "grp")), P(None, ("blk", "grp"))),
        check_vma=False,
    )
```

time: 1200 us -> 229 us (0.19)
  waiting for transfers between devices: 707 us -> 0 us
  matrix products: 275 us -> 0 us
  Pallas kernels: 0 us -> 222 us
  other arithmetic: 98.9 us -> 0 us
  local copies, waits for them, and re-layouts: 88.9 us -> 5.49 us
  between operations: 14.3 us -> 0.65 us
    reduce_scatter x1 -> x0, waiting for transfers between devices: 610 us -> none  [per_device(): lax.psum_scatter(partial_value, ('blk', 'grp'), scatter_dimension=1, tile...]
    dot_general x16 -> x0, matrix products: 275 us -> none  [block_terms(): lax.dot_general(adjoint, density, (((0,), (0,)), ((), ())), precision=HIGH)]
    pallas_call x0 -> x3, Pallas kernels: none -> 222 us  [the longest x1 173 us: pair_sums(): pl.pallas_call(pair_kernel, out_shape=[jax.ShapeDtypeStruct((3, tgt_count...]
    ppermute x16 -> x0, waiting for transfers between devices: 96.5 us -> none  [shifted(): lax.ppermute(x, axis, [(i, (i + by) % devices) for i in range(devices)])]
    gather x3 -> x0, local copies, waits for them, and re-layouts: 70.9 us -> none  [the longest x1 40.5 us: per_device(): pair_weight = near_coef * jnp.take(weight_t, local_pair, axis=0)]
    scatter-add x2 -> x0, other arithmetic: 51.4 us -> none  [the longest x1 26.3 us: per_device(): partial_value = partial_value.at[:, near_src].add(-pair_val)]
    reduce_sum x34 -> x0, other arithmetic: 39.2 us -> none  [the longest x32 35.7 us: block_terms(): grad_s = -jnp.stack([jnp.sum(gx, 0), jnp.sum(gy, 0), jnp.sum(gz, 0)])]
  transfers between devices with their start and end apart: 18 -> 0, of which waited for: 17 -> 0; matrix products, arithmetic and copies ran while one was open for 34% -> 0% of each run, Pallas kernels for 0% -> 0%
where the time goes in v1:
time: 229 us; the launch traced here: 228 us
  Pallas kernels  222 us (97%)
  local copies, waits for them, and re-layouts  5.49 us (2%)
    pallas_call x1, Pallas kernels, pair_sums(): pl.pallas_call(pair_kernel, out_shape=[jax.ShapeDtypeStruct((3, tgt_count...  173 us
    pallas_call x1, Pallas kernels, gather_sources(): pl.pallas_call(functools.partial(gather_kernel, n), out_shape=jax.ShapeDt...  34.2 us
    pallas_call x1, Pallas kernels, reduce_sources(): pl.pallas_call(functools.partial(reduce_kernel, n, groups), out_shape=jax...  15 us

profile of v1, /device:TPU:1, one launch (start us, length us, event | category | flops | bytes accessed | tf_op | source)
XLA Modules:
  0.0 228.5 jit_solution(5061859436476919925)
XLA Ops:
  0.6 1.4 copy.14.cond_scale
  2.0 2.9 %concatenate.3.own = f32[72,512]{1,0:T(8,128)} concatenate(f32[64,512]{1,0:T(8,128)} %param.19, f32[3,512]{1,0:T(4,128)} %param.16, f32[3,512]{1,0:T(4,128)} %param.17, f32[1,512]{1,0:T(1,128)} %bitcast.12, f32[1,512]{1,0:T(1,128)S(1)} %broadcast_in_dim.31), dimensions={0} | concatenate | bytes 294912 | tf_op jit(solution)/shard_map/concatenate | solution.py:403
  4.9 34.2 %shard_map.131.packs = f32[16,72,512]{2,1,0:T(8,128)} custom-call(f32[72,512]{1,0:T(8,128)} %concatenate.3.own), custom_call_target="tpu_custom_call" | custom-call | tf_op jit(solution)/shard_map/pallas_call | solution.py:324
  39.1 173.2 %shard_map.132 = (f32[3,4096]{1,0:T(4,128)}, f32[16,16,128]{2,1,0:T(8,128)}) custom-call(s32[4096]{0:T(1024)} %near_tgt.1, s32[4096]{0:T(1024)} %near_src.1, f32[3,4096]{1,0:T(4,128)} %tgt_pos.1, f32[1,4096]{1,0:T(1,128)} %bitcast.9, s32[1,4096]{1,0:T(1,128)} %bitcast.10, f32[64,4096]{1,0:T(8,128)} %adjoint.1, f32[64,1]{1,0:T(8,128)} %copy.14.cond_scale, ...), custom_call_target="tpu_custom_call" | custom-call | tf_op jit(solution)/shard_map/pallas_call | solution.py:270
  212.3 15.0 %shard_map.133 = f32[3,64]{1,0:T(4,128)} custom-call(f32[16,16,128]{2,1,0:T(8,128)} %get-tuple-element.5.sums), custom_call_target="tpu_custom_call" | custom-call | tf_op jit(solution)/shard_map/pallas_call | solution.py:380
  227.2 1.2 copy.16
  (1 shorter events, 0.0 us)

commit v2 on v1

--- a/solution.py
+++ b/solution.py
@@ -18,6 +18,8 @@
 PACK = 72
 BLOCK = 256
 CHUNK = 512
+PIECE = 32
+GROUP = 16
 SUM_ROWS = 16
 
 
@@ -83,10 +85,17 @@
     return radius, normal
 
 
-def pair_kernel(
+def pair_kernel(*refs):
+    pieces = CHUNK // PIECE
+    units = [pltpu.ACC(unit)((PIECE, BLOCK), F32) for unit in range(2) for _ in range(pieces + pieces // 2)]
+    pl.run_scoped(lambda *accs: pair_body(accs, *refs), *units)
+
+
+def pair_body(
+    accs,
     near_tgt, near_src, tgt_pos, tgt_area, tgt_cond, adjoint, cond_scale, near_tgt_row, near_src_row, near_coef, packs,
     tgt_out, src_out,
-    held, left_m, rhs_c, rhs_g, src_rows, src_table, spread, tgt_sum, src_sum, product, buf0, buf1,
+    held, left_m, right_m, src_rows, src_table, spread, tgt_sum, src_sum, product, buf0, buf1,
 ):
     tgt_count = tgt_pos.shape[1]
     parts, _, per = packs.shape
@@ -94,12 +103,16 @@
     halves = per // BLOCK
     blocks = total // BLOCK
     chunks = tgt_count // CHUNK
+    pairs = near_coef.shape[1]
+    first_target = (near_tgt[0] // tgt_count) * tgt_count
+
+    scales = jnp.transpose(jnp.broadcast_to(cond_scale[...], (LANES, LANES)))[0:WIDTH]
+    scales = jnp.concatenate([scales] * (CHUNK // LANES), axis=1)
 
     def target_prep(i, _):
         cols = pl.ds(pl.multiple_of(i * CHUNK, CHUNK), CHUNK)
-        cond = tgt_cond[:, cols]
-        hit = lax.broadcasted_iota(jnp.int32, (WIDTH, CHUNK), 0) == cond
-        weight = tgt_area[:, cols] * jnp.sum(jnp.where(hit, cond_scale[...], 0.0), axis=0, keepdims=True)
+        hit = lax.broadcasted_iota(jnp.int32, (WIDTH, CHUNK), 0) == tgt_cond[:, cols]
+        weight = tgt_area[:, cols] * jnp.sum(jnp.where(hit, scales, 0.0), axis=0, keepdims=True)
         stacked = jnp.concatenate([adjoint[:, cols] * weight, target_features(tgt_pos[:, cols])], axis=0)
         flat = jnp.transpose(stacked)
         held[cols, :] = flat
@@ -113,15 +126,32 @@
 
     lax.fori_loop(0, chunks, target_prep, 0)
 
-    feature = lax.broadcasted_iota(jnp.int32, (LANES, 3 * LANES), 0) - WIDTH
-    which = lax.broadcasted_iota(jnp.int32, (LANES, 3 * LANES), 1) // LANES
-    pick = (feature == 5 + which) | (feature == 16 + which) | (feature == 25 + which)
-    picker = pick.astype(F32).astype(BF16)
+    count = CHUNK // PIECE
+    half = count // 2
+    radius_acc, first_acc = accs[0:count], accs[count : count + half]
+    coupling_acc, second_acc = accs[count + half : 2 * count + half], accs[2 * count + half :]
+
+    feature = lax.broadcasted_iota(jnp.int32, (BLOCK, BLOCK), 0) - WIDTH
+    which = lax.broadcasted_iota(jnp.int32, (BLOCK, BLOCK), 1) // LANES
+    for unit in range(2):
+        axis = which + 2 * unit
+        pick = (feature == 5 + axis) | (feature == 16 + axis) | (feature == 25 + axis)
+        pltpu.matmul_push_rhs((pick & (axis < 3)).astype(F32).astype(BF16), 0, unit)
+    pltpu.matmul_acc_lhs(radius_acc[0], left_m[0:PIECE, :], load_staged_rhs=0)
+    pltpu.matmul_acc_lhs(coupling_acc[0], left_m[0:PIECE, :], load_staged_rhs=0)
+    pltpu.matmul_pop(radius_acc[0])
+    pltpu.matmul_pop(coupling_acc[0])
 
     def spread_prep(i, _):
-        cols = pl.ds(pl.multiple_of(i * CHUNK, CHUNK), CHUNK)
-        spread[cols, :] = jnp.dot(left_m[cols, 0:LANES], picker, preferred_element_type=F32)
-        tgt_sum[cols, :] = jnp.zeros((CHUNK, 3 * LANES), F32)
+        for p in range(count):
+            left = left_m[pl.ds(pl.multiple_of(i * CHUNK + p * PIECE, PIECE), PIECE), :]
+            pltpu.matmul_acc_lhs(radius_acc[p], left)
+            pltpu.matmul_acc_lhs(coupling_acc[p], left)
+        for p in range(count):
+            at = pl.ds(pl.multiple_of(i * CHUNK + p * PIECE, PIECE), PIECE)
+            spread[at, 0 : 2 * LANES] = pltpu.matmul_pop(radius_acc[p])
+            spread[at, 2 * LANES :] = pltpu.matmul_pop(coupling_acc[p])[:, 0:LANES]
+            tgt_sum[at, :] = jnp.zeros((PIECE, 3 * LANES), F32)
         return 0
 
     lax.fori_loop(0, chunks, spread_prep, 0)
@@ -138,17 +168,16 @@
             scaled = density * (pack[WIDTH + 6 : WIDTH + 7] * INV_FOUR_PI)
             high = scaled.astype(BF16)
             low = (scaled - high.astype(F32)).astype(BF16)
-            rhs_c[block, 0:WIDTH, :] = high
-            rhs_c[block, WIDTH : 2 * WIDTH, :] = zeros
-            rhs_c[block, 2 * WIDTH : 3 * WIDTH, :] = high
-            rhs_c[block, 3 * WIDTH : 4 * WIDTH, :] = low
             radius, normal = source_features(pos, nrm)
-            rhs_g[block, 0:WIDTH, 0:BLOCK] = zeros
-            rhs_g[block, 0:WIDTH, BLOCK : 2 * BLOCK] = zeros
-            rhs_g[block, WIDTH : 2 * WIDTH, 0:BLOCK] = radius.astype(BF16)
-            rhs_g[block, WIDTH : 2 * WIDTH, BLOCK : 2 * BLOCK] = normal.astype(BF16)
+            for q, quarters in enumerate((
+                (high, zeros, high, low),
+                (zeros, radius.astype(BF16), zeros, zeros),
+                (zeros, normal.astype(BF16), zeros, zeros),
+            )):
+                for r, quarter in enumerate(quarters):
+                    right_m[block, q, r * WIDTH : (r + 1) * WIDTH, :] = quarter
             src_rows[block] = pack[WIDTH : WIDTH + 8]
-            src_sum[block] = jnp.zeros((24, BLOCK), F32)
+            src_sum[block] = jnp.zeros(src_sum.shape[1:], F32)
             stacked = jnp.concatenate([density, rows([nrm], WIDTH)], axis=0)
             src_table[pl.ds(pl.multiple_of(block * BLOCK, BLOCK), BLOCK), :] = jnp.transpose(stacked)
         return 0
@@ -157,65 +186,105 @@
 
     steps = blocks * chunks
 
-    def products(k, buf):
-        b, i = k // chunks, lax.rem(k, chunks)
-        rows_at = pl.ds(pl.multiple_of(i * CHUNK, CHUNK), CHUNK)
-        buf[:, 0:BLOCK] = jnp.dot(left_m[rows_at, :], rhs_c[b], preferred_element_type=F32)
-        buf[:, BLOCK : 3 * BLOCK] = jnp.dot(left_m[rows_at, 0:LANES], rhs_g[b], preferred_element_type=F32)
-
-    def sums(k, buf):
-        b, i = k // chunks, lax.rem(k, chunks)
+    def where(k):
+        k = jnp.minimum(k, steps - 1)
+        return k // chunks, lax.rem(k, chunks)
+
+    def enter(e, k):
+        b, i = where(k)
+
+        def left(p):
+            return left_m[pl.ds(pl.multiple_of(i * CHUNK + p * PIECE, PIECE), PIECE), :]
+
+        if e == 0:
+            pltpu.matmul_push_rhs(right_m[b, 1], 0, 0)
+            pltpu.matmul_push_rhs(right_m[b, 0], 0, 1)
+        if e == count:
+            pltpu.matmul_push_rhs(right_m[b, 2], 1, 0)
+            pltpu.matmul_push_rhs(right_m[b, 2], 1, 1)
+        if e < count:
+            load = 0 if e == 0 else None
+            pltpu.matmul_acc_lhs(radius_acc[e], left(e), load_staged_rhs=load)
+            pltpu.matmul_acc_lhs(coupling_acc[e], left(e), load_staged_rhs=load)
+        else:
+            load = 1 if e == count else None
+            pltpu.matmul_acc_lhs(first_acc[e - count], left(e - count), load_staged_rhs=load)
+            pltpu.matmul_acc_lhs(second_acc[e - count], left(e - half), load_staged_rhs=load)
+
+    def leave(e, buf):
+        if e < count:
+            at = slice(e * PIECE, (e + 1) * PIECE)
+            buf[at, BLOCK : 2 * BLOCK] = pltpu.matmul_pop(radius_acc[e])
+            buf[at, 0:BLOCK] = pltpu.matmul_pop(coupling_acc[e])
+        else:
+            for p, acc in ((e - count, first_acc[e - count]), (e - half, second_acc[e - count])):
+                buf[p * PIECE : (p + 1) * PIECE, 2 * BLOCK : 3 * BLOCK] = pltpu.matmul_pop(acc)
+
+    events = count + half
+    per_step = pairs // steps
+
+    def pick_pair(p):
+        t = near_tgt[p] - first_target
+        product[pl.ds(p, 1), :] = held[pl.ds(t, 1), :] * src_table[pl.ds(near_src[p], 1), :]
+
+    def sums(k, buf, after):
+        b, i = where(k)
         base = i * CHUNK
         src = src_rows[b]
         wide = BLOCK // LANES
         lane = [slice(j * LANES, (j + 1) * LANES) for j in range(wide)]
         row = [[jnp.broadcast_to(src[q : q + 1, lane[j]], (8, LANES)) for q in range(6)] for j in range(wide)]
-        acc = [[src_sum[b, 8 * c : 8 * c + 8, lane[j]] for c in range(3)] for j in range(wide)]
-        for r in range(CHUNK // 8):
+        groups = CHUNK // 8
+        acc = None
+        for r in range(groups):
+            for e in range(events):
+                if e * groups // events == r:
+                    leave(e, after)
+                    enter(e, k + 2)
+            for u in range(per_step):
+                if u * groups // per_step == r:
+                    pick_pair(k * per_step + u)
+            if r % GROUP == 0:
+                acc = [[None] * 3 for _ in range(wide)]
             at = pl.ds(pl.multiple_of(base + 8 * r, 8), 8)
             here = [spread[at, c * LANES : (c + 1) * LANES] for c in range(3)]
             total_t = [None] * 3
             for j in range(wide):
-                coupling = buf[8 * r : 8 * r + 8, j * LANES : (j + 1) * LANES]
-                radius = buf[8 * r : 8 * r + 8, BLOCK + j * LANES : BLOCK + (j + 1) * LANES]
-                normal = buf[8 * r : 8 * r + 8, 2 * BLOCK + j * LANES : 2 * BLOCK + (j + 1) * LANES]
+                cols = slice(8 * r, 8 * r + 8)
+                coupling = buf[cols, j * LANES : (j + 1) * LANES]
+                radius = buf[cols, BLOCK + j * LANES : BLOCK + (j + 1) * LANES]
+                normal = buf[cols, 2 * BLOCK + j * LANES : 2 * BLOCK + (j + 1) * LANES]
                 inv = lax.rsqrt(radius)
                 inv2 = inv * inv
                 scale = (coupling * inv) * inv2
                 along = normal * inv2
                 for c in range(3):
                     g = scale * (row[j][3 + c] - along * (here[c] - row[j][c]))
-                    acc[j][c] = acc[j][c] + g
+                    acc[j][c] = g if acc[j][c] is None else acc[j][c] + g
                     total_t[c] = g if total_t[c] is None else total_t[c] + g
             for c in range(3):
                 tgt_sum[at, c * LANES : (c + 1) * LANES] += total_t[c]
-        for j in range(wide):
-            for c in range(3):
-                src_sum[b, 8 * c : 8 * c + 8, lane[j]] = acc[j][c]
-
-    products(0, buf0)
+            if r % GROUP == GROUP - 1:
+                for j in range(wide):
+                    for c in range(3):
+                        src_sum[b, r // GROUP, 8 * c : 8 * c + 8, lane[j]] += acc[j][c]
+
+    for e in range(events):
+        enter(e, 0)
+    for e in range(events):
+        leave(e, buf0)
+        enter(e, 1)
+
+    once = jnp.where(near_src[0] >= 0, 1, 0)
 
     def far(h, _):
-        k = 2 * h
-        products(k + 1, buf1)
-        sums(k, buf0)
-        products(jnp.minimum(k + 2, steps - 1), buf0)
-        sums(k + 1, buf1)
+        lax.fori_loop(0, once, lambda z, c: (sums(2 * h, buf0, buf1), c)[1], 0)
+        lax.fori_loop(0, once, lambda z, c: (sums(2 * h + 1, buf1, buf0), c)[1], 0)
         return 0
 
     lax.fori_loop(0, steps // 2, far, 0)
-
-    pairs = near_coef.shape[1]
-    first_target = (near_tgt[0] // tgt_count) * tgt_count
-
-    def gather(i, _):
-        for u in range(16):
-            p = i * 16 + u
-            t = near_tgt[p] - first_target
-            product[pl.ds(p, 1), :] = held[pl.ds(t, 1), :] * src_table[pl.ds(near_src[p], 1), :]
-        return 0
-
-    lax.fori_loop(0, pairs // 16, gather, 0)
+    for e in range(events):
+        leave(e, buf0)
 
     flat = jnp.transpose(product[...])
     coupled = jnp.sum(flat[0:WIDTH], axis=0, keepdims=True) * near_coef[...]
@@ -223,17 +292,27 @@
     high = part(value)
     both = rows([high, part(value - high)], 8)
 
-    def scatter(index, groups):
-        row_at, lane_at = index // LANES, lax.rem(index, LANES)
-        chosen = [jnp.where(row_at == g, both, 0.0).astype(BF16) for g in range(groups)]
-        lanes = (lax.broadcasted_iota(jnp.int32, (LANES, pairs), 0) == lane_at).astype(F32).astype(BF16)
-        return lax.dot_general(
-            jnp.concatenate(chosen, axis=0), lanes, (((1,), (1,)), ((), ())), preferred_element_type=F32
-        )
+    def scatter(index, unit, acc):
+        row_at, lane_at = index // BLOCK, lax.rem(index, BLOCK)
+        picked = [jnp.where(row_at == g, both, 0.0) for g in range(4 * len(acc))]
+        picked = jnp.concatenate(picked, axis=0).astype(BF16)
+        lanes = (lax.broadcasted_iota(jnp.int32, (BLOCK, pairs), 0) == lane_at).astype(F32).astype(BF16)
+        for q in range(pairs // BLOCK):
+            at = slice(q * BLOCK, (q + 1) * BLOCK)
+            pltpu.matmul_push_rhs(lanes[:, at], q % 2, unit, transpose=True)
+            for p in range(len(acc)):
+                load = q % 2 if p == 0 else None
+                pltpu.matmul_acc_lhs(acc[p], picked[p * PIECE : (p + 1) * PIECE, at], load_staged_rhs=load)
+        return jnp.concatenate([pltpu.matmul_pop(one) for one in acc], axis=0)
 
     local = near_tgt_row[...] - first_target
-    to_tgt = scatter(local, tgt_count // LANES)
-    to_src = scatter(near_src_row[...], total // LANES)
+    to_tgt = scatter(local, 0, radius_acc[0 : tgt_count // BLOCK // 4])
+    to_src = scatter(near_src_row[...], 1, coupling_acc[0 : total // BLOCK // 4])
+    wide = BLOCK // LANES
+
+    def near_of(sums_by_row, g):
+        near = sums_by_row[8 * (g // wide) : 8 * (g // wide) + 8, g % wide * LANES : (g % wide + 1) * LANES]
+        return near[0:3] + near[3:6]
 
     lane = lax.broadcasted_iota(jnp.int32, (LANES, LANES), 1)
     for g in range(tgt_count // LANES):
@@ -242,19 +321,18 @@
         for c in range(3):
             one = jnp.sum(tgt_sum[at, c * LANES : (c + 1) * LANES], axis=1, keepdims=True)
             merged = jnp.where(lane == c, one, merged)
-        near = to_tgt[8 * g : 8 * g + 8]
-        tgt_out[:, at] = jnp.transpose(merged)[0:3] + near[0:3] + near[3:6]
+        tgt_out[:, at] = jnp.transpose(merged)[0:3] + near_of(to_tgt, g)
     quarters = per // LANES
     for b in range(parts):
         src_out[b, 3 * quarters :, :] = jnp.zeros((src_out.shape[1] - 3 * quarters, LANES), F32)
         for q in range(quarters):
             g = b * quarters + q
             block, j = divmod(g, BLOCK // LANES)
-            near = to_src[8 * g : 8 * g + 8]
-            near = near[0:3] + near[3:6]
+            near = near_of(to_src, g)
             at = slice(j * LANES, (j + 1) * LANES)
+            together = sum(src_sum[block, s, :, at] for s in range(src_sum.shape[1]))
             for c in range(3):
-                far_sum = jnp.sum(src_sum[block, 8 * c : 8 * c + 8, at], axis=0, keepdims=True)
+                far_sum = jnp.sum(together[8 * c : 8 * c + 8], axis=0, keepdims=True)
                 row = c * quarters + q
                 src_out[b, row : row + 1, :] = -far_sum - near[c : c + 1]
 
@@ -269,26 +347,28 @@
     smem = pl.BlockSpec(memory_space=pltpu.SMEM)
     return pl.pallas_call(
         pair_kernel,
-        out_shape=[jax.ShapeDtypeStruct((3, tgt_count), F32), jax.ShapeDtypeStruct((parts, SUM_ROWS, LANES), F32)],
+        out_shape=[
+            jax.ShapeDtypeStruct((3, tgt_count), F32),
+            jax.ShapeDtypeStruct((parts, SUM_ROWS, LANES), F32),
+        ],
         in_specs=[smem, smem] + [vmem] * 9,
         out_specs=[vmem, vmem],
         scratch_shapes=[
             pltpu.VMEM((tgt_count, LANES), F32),
             pltpu.VMEM((tgt_count, 2 * LANES), BF16),
-            pltpu.VMEM((blocks, 4 * WIDTH, BLOCK), BF16),
-            pltpu.VMEM((blocks, 2 * WIDTH, 2 * BLOCK), BF16),
+            pltpu.VMEM((blocks, 3, BLOCK, BLOCK), BF16),
             pltpu.VMEM((blocks, 8, BLOCK), F32),
             pltpu.VMEM((total, LANES), F32),
             pltpu.VMEM((tgt_count, 3 * LANES), F32),
             pltpu.VMEM((tgt_count, 3 * LANES), F32),
-            pltpu.VMEM((blocks, 24, BLOCK), F32),
+            pltpu.VMEM((blocks, CHUNK // 8 // GROUP, 24, BLOCK), F32),
             pltpu.VMEM((pairs, LANES), F32),
             pltpu.VMEM((CHUNK, 3 * BLOCK), F32),
             pltpu.VMEM((CHUNK, 3 * BLOCK), F32),
         ],
         compiler_params=pltpu.CompilerParams(vmem_limit_bytes=60 * 2**20),
     )(
-        near_tgt, near_src, tgt_pos, tgt_area[None, :], tgt_cond[None, :], adjoint, cond_scale[:, None],
+        near_tgt, near_src, tgt_pos, tgt_area[None, :], tgt_cond[None, :], adjoint, jnp.pad(cond_scale, (0, LANES - WIDTH))[None, :],
         near_tgt[None, :], near_src[None, :], near_coef[None, :], packs,
     )
 
@@ -300,39 +380,93 @@
     pl.semaphore_wait(barrier, len(peers))
 
 
-def gather_kernel(n, own, out, send_sem, recv_sem, local_sem):
-    me = lax.axis_index("blk")
-    others = [lax.rem(me + k, n) for k in range(1, n)]
-    greet([{"blk": other} for other in others])
-    copies = []
-    for k, other in enumerate(others):
+def gather_kernel(density, pos, nrm, area, out, pack, send_sem, recv_sem, local_sem):
+    me, grp = lax.axis_index("blk"), lax.axis_index("grp")
+    z, y_lo, core = me // 4, lax.rem(me // 2, 2), lax.rem(me, 2)
+
+    def block(z_at, y_at, core_at):
+        return (lax.rem(z_at, 4) * 2 + y_at) * 2 + core_at
+
+    up, down = block(z + 1, y_lo, core), block(z + 3, y_lo, core)
+    beside, mate = block(z, 1 - y_lo, core), block(z, y_lo, 1 - core)
+    other = grp + 1 - 2 * lax.rem(grp, 2)
+    to_up, to_down, to_mate = {"blk": up}, {"blk": down}, {"blk": mate}
+    to_beside, to_around = {"blk": beside}, {"blk": beside, "grp": other}
+
+    width = density.shape[0]
+    pack[0:width, :] = density[...]
+    pack[width:, :] = jnp.concatenate(
+        [pos[...], nrm[...], area[...], jnp.zeros((PACK - width - 7, pos.shape[1]), F32)], axis=0
+    )
+    greet([to_up, to_down, to_mate, to_beside, to_around])
+
+    whole, first, second = pl.ds(0, PACK), pl.ds(0, 40), pl.ds(40, PACK - 40)
+    copies = {}
+
+    def send(name, source, piece, device):
+        k = len(copies)
+        held = pack if source is me else out.at[source]
         copy = pltpu.make_async_remote_copy(
-            src_ref=own, dst_ref=out.at[me], send_sem=send_sem.at[k], recv_sem=recv_sem.at[k],
-            device_id={"blk": other}, device_id_type=MESH,
+            src_ref=held.at[piece], dst_ref=out.at[source, piece], send_sem=send_sem.at[k], recv_sem=recv_sem.at[k],
+            device_id=device, device_id_type=MESH,
         )
         copy.start()
-        copies.append(copy)
-    mine = pltpu.make_async_copy(own, out.at[me], local_sem)
+        copies[name] = copy
+
+    def spread_y(name, source):
+        send(name + "first", source, first, to_beside)
+        send(name + "second", source, second, to_around)
+
+    def arrived(*names):
+        for name in names:
+            copies[name].wait_recv()
+
+    send("up", me, whole, to_up)
+    send("down", me, whole, to_down)
+    spread_y("y0", me)
+    send("c0", me, whole, to_mate)
+    mine = pltpu.make_async_copy(pack, out.at[me], local_sem)
     mine.start()
+    arrived("up")
+    send("up2", down, first, to_up)
+    spread_y("y3", down)
+    send("c3", down, whole, to_mate)
+    arrived("down")
+    send("down2", up, second, to_down)
+    spread_y("y1", up)
+    send("c1", up, whole, to_mate)
+    across = block(z + 2, y_lo, core)
+    arrived("up2", "down2")
+    spread_y("y2", across)
+    send("c2", across, whole, to_mate)
+    for step in (0, 3, 1, 2):
+        arrived("y%dfirst" % step, "y%dsecond" % step)
+        send("cy%d" % step, block(z + step, 1 - y_lo, core), whole, to_mate)
+    for step in (0, 3, 1, 2):
+        arrived("c%d" % step)
+    for step in (0, 3, 1, 2):
+        arrived("cy%d" % step)
     mine.wait()
-    for copy in copies:
-        copy.wait()
-
-
-def gather_sources(pack, n):
-    hbm = pl.BlockSpec(memory_space=pl.ANY)
+    for copy in copies.values():
+        copy.wait_send()
+
+
+def gather_sources(density, pos, nrm, area, n):
+    vmem, hbm = pl.BlockSpec(memory_space=pltpu.VMEM), pl.BlockSpec(memory_space=pl.ANY)
+    shape = (PACK, pos.shape[1])
     return pl.pallas_call(
-        functools.partial(gather_kernel, n),
-        out_shape=jax.ShapeDtypeStruct((n,) + pack.shape, F32),
-        in_specs=[hbm],
+        gather_kernel,
+        out_shape=jax.ShapeDtypeStruct((n,) + shape, F32),
+        in_specs=[vmem] * 4,
         out_specs=hbm,
         scratch_shapes=[
-            pltpu.SemaphoreType.DMA((n - 1,)),
-            pltpu.SemaphoreType.DMA((n - 1,)),
+            pltpu.VMEM(shape, F32),
+            pltpu.SemaphoreType.DMA((20,)),
+            pltpu.SemaphoreType.DMA((20,)),
             pltpu.SemaphoreType.DMA,
         ],
         compiler_params=pltpu.CompilerParams(collective_id=0, has_side_effects=True),
-    )(pack)
+    )(density, pos, nrm, area[None, :])
 
 
 def reduce_kernel(n, groups, sums, out, first, second, mine, send1, recv1, send2, recv2):
@@ -399,9 +533,7 @@
     tgt_pos, tgt_area, tgt_cond, adjoint, src_pos, src_nrm, src_area, density, cond_scale, near_tgt, near_src, near_coef
 ):
     n, groups = lax.axis_size("blk"), lax.axis_size("grp")
-    filler = jnp.zeros((PACK - WIDTH - 7, src_pos.shape[1]), F32)
-    pack = jnp.concatenate([density, src_pos, src_nrm, src_area[None, :], filler], axis=0)
-    packs = gather_sources(pack, n)
+    packs = gather_sources(density, src_pos, src_nrm, src_area, n)
     tgt_grad, sums = pair_sums(
         tgt_pos, tgt_area, tgt_cond, adjoint, cond_scale, near_tgt, near_src, near_coef, packs
     )

time: 229 us -> 183 us (0.80)
  Pallas kernels: 222 us -> 180 us
  local copies, waits for them, and re-layouts: 5.49 us -> 2.42 us
    pallas_call x1, Pallas kernels: 173 us -> 144 us  [pair_sums(): pl.pallas_call(pair_kernel, out_shape=[jax.ShapeDtypeStruct((3, tgt_count...]
    pallas_call x1, Pallas kernels: 34.2 us -> 22.1 us  [gather_sources(): pl.pallas_call(gather_kernel, out_shape=jax.ShapeDtypeStruct((n,) + shape...]
    concatenate x1 -> x0, local copies, waits for them, and re-layouts: 2.89 us -> none  [per_device(): jnp.concatenate([density, src_pos, src_nrm, src_area[None, :], filler], a...]
where the time goes in v2:
time: 183 us
  Pallas kernels  180 us (98%)
  local copies, waits for them, and re-layouts  2.42 us (1%)
    pallas_call x1, Pallas kernels, pair_sums(): pl.pallas_call(pair_kernel, out_shape=[jax.ShapeDtypeStruct((3, tgt_count...  144 us
    pallas_call x1, Pallas kernels, gather_sources(): pl.pallas_call(gather_kernel, out_shape=jax.ShapeDtypeStruct((n,) + shape...  22.1 us
    pallas_call x1, Pallas kernels, reduce_sources(): pl.pallas_call(functools.partial(reduce_kernel, n, groups), out_shape=jax...  14.3 us

profile of v2, /device:TPU:1, one launch (start us, length us, event | category | flops | bytes accessed | tf_op | source)
XLA Modules:
  0.0 183.1 jit_solution(9637928826018535927)
XLA Ops:
  0.6 1.2 pad_bitcast_fusion.refs_6_
  1.8 22.1 %shard_map.131.refs_10_ = f32[16,72,512]{2,1,0:T(8,128)} custom-call(f32[64,512]{1,0:T(8,128)} %density.1, f32[3,512]{1,0:T(4,128)} %pos.1, f32[3,512]{1,0:T(4,128)} %nrm.1, f32[1,512]{1,0:T(1,128)} %bitcast.13), custom_call_target="tpu_custom_call" | custom-call | tf_op jit(solution)/shard_map/pallas_call | solution.py:457
  23.9 143.6 %shard_map.132 = (f32[3,4096]{1,0:T(4,128)}, f32[16,16,128]{2,1,0:T(8,128)}) custom-call(s32[4096]{0:T(1024)} %refs_0_.1, s32[4096]{0:T(1024)} %refs_1_.1, f32[3,4096]{1,0:T(4,128)} %refs_2_.1, f32[1,4096]{1,0:T(1,128)} %bitcast.10, s32[1,4096]{1,0:T(1,128)} %bitcast.11, f32[64,4096]{1,0:T(8,128)} %refs_5_.1, f32[1,128]{1,0:T(1,128)} %pad_bitcast_fusion.refs_6_, ...), custom_call_target="tpu_custom_call" | custom-call | tf_op jit(solution)/shard_map/pallas_call | solution.py:348
  167.5 14.3 %shard_map.133 = f32[3,64]{1,0:T(4,128)} custom-call(f32[16,16,128]{2,1,0:T(8,128)} %get-tuple-element.5.sums), custom_call_target="tpu_custom_call" | custom-call | tf_op jit(solution)/shard_map/pallas_call | solution.py:514
  181.9 1.2 copy.15

commit v3 on v2

--- a/solution.py
+++ b/solution.py
@@ -19,7 +19,7 @@
 BLOCK = 256
 CHUNK = 512
 PIECE = 32
-GROUP = 16
+GROUP = 32
 SUM_ROWS = 16
 
 
@@ -93,10 +93,12 @@
 
 def pair_body(
     accs,
-    near_tgt, near_src, tgt_pos, tgt_area, tgt_cond, adjoint, cond_scale, near_tgt_row, near_src_row, near_coef, packs,
+    near_tgt, near_src, tgt_pos, tgt_area, tgt_cond, adjoint, cond_scale, near_tgt_row, near_src_row, near_coef, packs_in,
     tgt_out, src_out,
-    held, left_m, right_m, src_rows, src_table, spread, tgt_sum, src_sum, product, buf0, buf1,
+    packs, packs_sem, held, left_m, right_m, src_rows, src_table, spread, tgt_sum, src_sum, product, buf0, buf1,
 ):
+    fetch = pltpu.make_async_copy(packs_in, packs, packs_sem)
+    fetch.start()
     tgt_count = tgt_pos.shape[1]
     parts, _, per = packs.shape
     total = parts * per
@@ -106,7 +108,8 @@
     pairs = near_coef.shape[1]
     first_target = (near_tgt[0] // tgt_count) * tgt_count
 
-    scales = jnp.transpose(jnp.broadcast_to(cond_scale[...], (LANES, LANES)))[0:WIDTH]
+    scales = jnp.concatenate([cond_scale[...], jnp.zeros((1, LANES - WIDTH), F32)], axis=1)
+    scales = jnp.transpose(jnp.broadcast_to(scales, (LANES, LANES)))[0:WIDTH]
     scales = jnp.concatenate([scales] * (CHUNK // LANES), axis=1)
 
     def target_prep(i, _):
@@ -182,6 +185,7 @@
             src_table[pl.ds(pl.multiple_of(block * BLOCK, BLOCK), BLOCK), :] = jnp.transpose(stacked)
         return 0
 
+    fetch.wait()
     lax.fori_loop(0, parts, source_prep, 0)
 
     steps = blocks * chunks
@@ -190,35 +194,29 @@
         k = jnp.minimum(k, steps - 1)
         return k // chunks, lax.rem(k, chunks)
 
-    def enter(e, k):
+    def turn(e, unit, odd):
+        if unit == 0:
+            whole = [(1, p, radius_acc[p]) for p in range(count)]
+            part_of = [(2, p, first_acc[p]) for p in range(half)]
+        else:
+            whole = [(0, p, coupling_acc[p]) for p in range(count)]
+            part_of = [(2, p + half, second_acc[p]) for p in range(half)]
+        order = whole + part_of if unit == odd else part_of + whole
+        change = len(whole) if unit == odd else len(part_of)
+        return order[e] + (e == change or (e == 0 and odd == 0),)
+
+    def enter(e, k, unit, odd):
         b, i = where(k)
-
-        def left(p):
-            return left_m[pl.ds(pl.multiple_of(i * CHUNK + p * PIECE, PIECE), PIECE), :]
-
-        if e == 0:
-            pltpu.matmul_push_rhs(right_m[b, 1], 0, 0)
-            pltpu.matmul_push_rhs(right_m[b, 0], 0, 1)
-        if e == count:
-            pltpu.matmul_push_rhs(right_m[b, 2], 1, 0)
-            pltpu.matmul_push_rhs(right_m[b, 2], 1, 1)
-        if e < count:
-            load = 0 if e == 0 else None
-            pltpu.matmul_acc_lhs(radius_acc[e], left(e), load_staged_rhs=load)
-            pltpu.matmul_acc_lhs(coupling_acc[e], left(e), load_staged_rhs=load)
-        else:
-            load = 1 if e == count else None
-            pltpu.matmul_acc_lhs(first_acc[e - count], left(e - count), load_staged_rhs=load)
-            pltpu.matmul_acc_lhs(second_acc[e - count], left(e - half), load_staged_rhs=load)
-
-    def leave(e, buf):
-        if e < count:
-            at = slice(e * PIECE, (e + 1) * PIECE)
-            buf[at, BLOCK : 2 * BLOCK] = pltpu.matmul_pop(radius_acc[e])
-            buf[at, 0:BLOCK] = pltpu.matmul_pop(coupling_acc[e])
-        else:
-            for p, acc in ((e - count, first_acc[e - count]), (e - half, second_acc[e - count])):
-                buf[p * PIECE : (p + 1) * PIECE, 2 * BLOCK : 3 * BLOCK] = pltpu.matmul_pop(acc)
+        matrix, p, acc, first = turn(e, unit, odd)
+        staged = 1 if matrix == 2 else 0
+        if first:
+            pltpu.matmul_push_rhs(right_m[b, matrix], staged, unit)
+        left = left_m[pl.ds(pl.multiple_of(i * CHUNK + p * PIECE, PIECE), PIECE), :]
+        pltpu.matmul_acc_lhs(acc, left, load_staged_rhs=staged if first else None)
+
+    def leave(e, buf, unit, odd):
+        matrix, p, acc, _ = turn(e, unit, odd)
+        buf[p * PIECE : (p + 1) * PIECE, matrix * BLOCK : (matrix + 1) * BLOCK] = pltpu.matmul_pop(acc)
 
     events = count + half
     per_step = pairs // steps
@@ -227,7 +225,7 @@
         t = near_tgt[p] - first_target
         product[pl.ds(p, 1), :] = held[pl.ds(t, 1), :] * src_table[pl.ds(near_src[p], 1), :]
 
-    def sums(k, buf, after):
+    def sums(k, buf, after, odd):
         b, i = where(k)
         base = i * CHUNK
         src = src_rows[b]
@@ -237,10 +235,11 @@
         groups = CHUNK // 8
         acc = None
         for r in range(groups):
-            for e in range(events):
-                if e * groups // events == r:
-                    leave(e, after)
-                    enter(e, k + 2)
+            for unit in range(2):
+                for e in range(events):
+                    if (2 * e + unit) * groups // (2 * events) == r:
+                        leave(e, after, unit, odd)
+                        enter(e, k + 2, unit, odd)
             for u in range(per_step):
                 if u * groups // per_step == r:
                     pick_pair(k * per_step + u)
@@ -269,22 +268,25 @@
                     for c in range(3):
                         src_sum[b, r // GROUP, 8 * c : 8 * c + 8, lane[j]] += acc[j][c]
 
-    for e in range(events):
-        enter(e, 0)
-    for e in range(events):
-        leave(e, buf0)
-        enter(e, 1)
+    for unit in range(2):
+        for e in range(events):
+            enter(e, 0, unit, 0)
+    for unit in range(2):
+        for e in range(events):
+            leave(e, buf0, unit, 1)
+            enter(e, 1, unit, 1)
 
     once = jnp.where(near_src[0] >= 0, 1, 0)
 
     def far(h, _):
-        lax.fori_loop(0, once, lambda z, c: (sums(2 * h, buf0, buf1), c)[1], 0)
-        lax.fori_loop(0, once, lambda z, c: (sums(2 * h + 1, buf1, buf0), c)[1], 0)
+        lax.fori_loop(0, once, lambda z, c: (sums(2 * h, buf0, buf1, 0), c)[1], 0)
+        lax.fori_loop(0, once, lambda z, c: (sums(2 * h + 1, buf1, buf0, 1), c)[1], 0)
         return 0
 
     lax.fori_loop(0, steps // 2, far, 0)
-    for e in range(events):
-        leave(e, buf0)
+    for unit in range(2):
+        for e in range(events):
+            leave(e, buf0, unit, 0)
 
     flat = jnp.transpose(product[...])
     coupled = jnp.sum(flat[0:WIDTH], axis=0, keepdims=True) * near_coef[...]
@@ -351,9 +353,11 @@
             jax.ShapeDtypeStruct((3, tgt_count), F32),
             jax.ShapeDtypeStruct((parts, SUM_ROWS, LANES), F32),
         ],
-        in_specs=[smem, smem] + [vmem] * 9,
+        in_specs=[smem, smem] + [vmem] * 8 + [pl.BlockSpec(memory_space=pl.ANY)],
         out_specs=[vmem, vmem],
         scratch_shapes=[
+            pltpu.VMEM(packs.shape, F32),
+            pltpu.SemaphoreType.DMA,
             pltpu.VMEM((tgt_count, LANES), F32),
             pltpu.VMEM((tgt_count, 2 * LANES), BF16),
             pltpu.VMEM((blocks, 3, BLOCK, BLOCK), BF16),
@@ -368,7 +372,7 @@
         ],
         compiler_params=pltpu.CompilerParams(vmem_limit_bytes=60 * 2**20),
     )(
-        near_tgt, near_src, tgt_pos, tgt_area[None, :], tgt_cond[None, :], adjoint, jnp.pad(cond_scale, (0, LANES - WIDTH))[None, :],
+        near_tgt, near_src, tgt_pos, tgt_area[None, :], tgt_cond[None, :], adjoint, cond_scale[None, :],
         near_tgt[None, :], near_src[None, :], near_coef[None, :], packs,
     )
 
@@ -413,34 +417,39 @@
         copy.start()
         copies[name] = copy
 
-    def spread_y(name, source):
-        send(name + "first", source, first, to_beside)
-        send(name + "second", source, second, to_around)
-
     def arrived(*names):
         for name in names:
             copies[name].wait_recv()
 
-    send("up", me, whole, to_up)
-    send("down", me, whole, to_down)
-    spread_y("y0", me)
+    across = block(z + 2, y_lo, core)
+    send("up1", me, first, to_up)
+    send("down1", me, second, to_down)
+    send("y0a", me, first, to_beside)
+    send("y0b", me, second, to_around)
+    send("up2", me, second, to_up)
+    send("down2", me, first, to_down)
     send("c0", me, whole, to_mate)
     mine = pltpu.make_async_copy(pack, out.at[me], local_sem)
     mine.start()
-    arrived("up")
-    send("up2", down, first, to_up)
-    spread_y("y3", down)
+    arrived("up1")
+    send("on_up", down, first, to_up)
+    send("y3a", down, first, to_beside)
+    arrived("down1")
+    send("on_down", up, second, to_down)
+    send("y1b", up, second, to_around)
+    arrived("up2")
+    send("y3b", down, second, to_around)
+    arrived("down2")
+    send("y1a", up, first, to_beside)
     send("c3", down, whole, to_mate)
-    arrived("down")
-    send("down2", up, second, to_down)
-    spread_y("y1", up)
     send("c1", up, whole, to_mate)
-    across = block(z + 2, y_lo, core)
-    arrived("up2", "down2")
-    spread_y("y2", across)
+    arrived("on_up")
+    send("y2a", across, first, to_beside)
+    arrived("on_down")
+    send("y2b", across, second, to_around)
     send("c2", across, whole, to_mate)
     for step in (0, 3, 1, 2):
-        arrived("y%dfirst" % step, "y%dsecond" % step)
+        arrived("y%da" % step, "y%db" % step)
         send("cy%d" % step, block(z + step, 1 - y_lo, core), whole, to_mate)
     for step in (0, 3, 1, 2):
         arrived("c%d" % step)
@@ -461,8 +470,8 @@
         out_specs=hbm,
         scratch_shapes=[
             pltpu.VMEM(shape, F32),
-            pltpu.SemaphoreType.DMA((20,)),
-            pltpu.SemaphoreType.DMA((20,)),
+            pltpu.SemaphoreType.DMA((22,)),
+            pltpu.SemaphoreType.DMA((22,)),
             pltpu.SemaphoreType.DMA,
         ],
         compiler_params=pltpu.CompilerParams(collective_id=0, has_side_effects=True),

time: 183 us -> 172 us (0.940)
  Pallas kernels: 180 us -> 170 us
    pallas_call x1, Pallas kernels: 144 us -> 135 us  [pair_sums(): pl.pallas_call(pair_kernel, out_shape=[jax.ShapeDtypeStruct((3, tgt_count...]
where the time goes in v3:
time: 172 us
  Pallas kernels  170 us (99%)
    pallas_call x1, Pallas kernels, pair_sums(): pl.pallas_call(pair_kernel, out_shape=[jax.ShapeDtypeStruct((3, tgt_count...  135 us
    pallas_call x1, Pallas kernels, gather_sources(): pl.pallas_call(gather_kernel, out_shape=jax.ShapeDtypeStruct((n,) + shape...  21.7 us
    pallas_call x1, Pallas kernels, reduce_sources(): pl.pallas_call(functools.partial(reduce_kernel, n, groups), out_shape=jax...  14.1 us

profile of v3, /device:TPU:1, one launch (start us, length us, event | category | flops | bytes accessed | tf_op | source)
XLA Modules:
  0.0 172.3 jit_solution(463701044304729585)
XLA Ops:
  0.6 21.7 %shard_map.131.refs_10_ = f32[16,72,512]{2,1,0:T(8,128)} custom-call(f32[64,512]{1,0:T(8,128)} %density.1, f32[3,512]{1,0:T(4,128)} %pos.1, f32[3,512]{1,0:T(4,128)} %nrm.1, f32[1,512]{1,0:T(1,128)} %bitcast.12), custom_call_target="tpu_custom_call" | custom-call | tf_op jit(solution)/shard_map/pallas_call | solution.py:466
  22.3 134.6 %shard_map.132 = (f32[3,4096]{1,0:T(4,128)}, f32[16,16,128]{2,1,0:T(8,128)}) custom-call(s32[4096]{0:T(1024)} %refs_0_.1, s32[4096]{0:T(1024)} %refs_1_.1, f32[3,4096]{1,0:T(4,128)} %refs_2_.1, f32[1,4096]{1,0:T(1,128)} %bitcast.9, s32[1,4096]{1,0:T(1,128)} %bitcast.10, f32[64,4096]{1,0:T(8,128)} %refs_5_.1, f32[1,64]{1,0:T(1,128)} %bitcast.13, ...), custom_call_target="tpu_custom_call" | custom-call | tf_op jit(solution)/shard_map/pallas_call | solution.py:350
  156.9 14.1 %shard_map.133 = f32[3,64]{1,0:T(4,128)} custom-call(f32[16,16,128]{2,1,0:T(8,128)} %get-tuple-element.5.sums), custom_call_target="tpu_custom_call" | custom-call | tf_op jit(solution)/shard_map/pallas_call | solution.py:523
  171.0 1.2 copy.15

commit v4 on v3

--- a/solution.py
+++ b/solution.py
@@ -19,7 +19,7 @@
 BLOCK = 256
 CHUNK = 512
 PIECE = 32
-GROUP = 32
+GROUP = 64
 SUM_ROWS = 16
 
 
@@ -85,29 +85,7 @@
     return radius, normal
 
 
-def pair_kernel(*refs):
-    pieces = CHUNK // PIECE
-    units = [pltpu.ACC(unit)((PIECE, BLOCK), F32) for unit in range(2) for _ in range(pieces + pieces // 2)]
-    pl.run_scoped(lambda *accs: pair_body(accs, *refs), *units)
-
-
-def pair_body(
-    accs,
-    near_tgt, near_src, tgt_pos, tgt_area, tgt_cond, adjoint, cond_scale, near_tgt_row, near_src_row, near_coef, packs_in,
-    tgt_out, src_out,
-    packs, packs_sem, held, left_m, right_m, src_rows, src_table, spread, tgt_sum, src_sum, product, buf0, buf1,
-):
-    fetch = pltpu.make_async_copy(packs_in, packs, packs_sem)
-    fetch.start()
-    tgt_count = tgt_pos.shape[1]
-    parts, _, per = packs.shape
-    total = parts * per
-    halves = per // BLOCK
-    blocks = total // BLOCK
-    chunks = tgt_count // CHUNK
-    pairs = near_coef.shape[1]
-    first_target = (near_tgt[0] // tgt_count) * tgt_count
-
+def prepare_targets(start, stop, tgt_pos, tgt_area, tgt_cond, adjoint, cond_scale, held, left_m):
     scales = jnp.concatenate([cond_scale[...], jnp.zeros((1, LANES - WIDTH), F32)], axis=1)
     scales = jnp.transpose(jnp.broadcast_to(scales, (LANES, LANES)))[0:WIDTH]
     scales = jnp.concatenate([scales] * (CHUNK // LANES), axis=1)
@@ -127,37 +105,41 @@
         left_m[cols, LANES : 2 * LANES] = second.astype(BF16)
         return 0
 
-    lax.fori_loop(0, chunks, target_prep, 0)
+    lax.fori_loop(start, stop, target_prep, 0)
+
+
+def pair_kernel(*refs):
+    pieces = CHUNK // PIECE
+    units = [pltpu.ACC(unit)((PIECE, BLOCK), F32) for unit in range(2) for _ in range(pieces + pieces // 2)]
+    pl.run_scoped(lambda *accs: pair_body(accs, *refs), *units)
+
+
+def pair_body(
+    accs,
+    near_tgt_in, near_src_in, near_tgt_row, near_src_row, near_coef, held_in, left_in, packs_in,
+    tgt_out, src_out,
+    held, left_m, packs, near_tgt, near_src, sems, right_m, src_rows, src_table, spread, tgt_sum, src_sum, product, buf0, buf1,
+):
+    fetches = [
+        pltpu.make_async_copy(source, here, sems.at[q])
+        for q, (source, here) in enumerate(
+            ((packs_in, packs), (left_in, left_m), (held_in, held), (near_tgt_in, near_tgt), (near_src_in, near_src))
+        )
+    ]
+    for fetch in fetches:
+        fetch.start()
+    tgt_count = held.shape[0]
+    parts, _, per = packs.shape
+    total = parts * per
+    halves = per // BLOCK
+    blocks = total // BLOCK
+    chunks = tgt_count // CHUNK
+    pairs = near_coef.shape[1]
 
     count = CHUNK // PIECE
     half = count // 2
     radius_acc, first_acc = accs[0:count], accs[count : count + half]
     coupling_acc, second_acc = accs[count + half : 2 * count + half], accs[2 * count + half :]
-
-    feature = lax.broadcasted_iota(jnp.int32, (BLOCK, BLOCK), 0) - WIDTH
-    which = lax.broadcasted_iota(jnp.int32, (BLOCK, BLOCK), 1) // LANES
-    for unit in range(2):
-        axis = which + 2 * unit
-        pick = (feature == 5 + axis) | (feature == 16 + axis) | (feature == 25 + axis)
-        pltpu.matmul_push_rhs((pick & (axis < 3)).astype(F32).astype(BF16), 0, unit)
-    pltpu.matmul_acc_lhs(radius_acc[0], left_m[0:PIECE, :], load_staged_rhs=0)
-    pltpu.matmul_acc_lhs(coupling_acc[0], left_m[0:PIECE, :], load_staged_rhs=0)
-    pltpu.matmul_pop(radius_acc[0])
-    pltpu.matmul_pop(coupling_acc[0])
-
-    def spread_prep(i, _):
-        for p in range(count):
-            left = left_m[pl.ds(pl.multiple_of(i * CHUNK + p * PIECE, PIECE), PIECE), :]
-            pltpu.matmul_acc_lhs(radius_acc[p], left)
-            pltpu.matmul_acc_lhs(coupling_acc[p], left)
-        for p in range(count):
-            at = pl.ds(pl.multiple_of(i * CHUNK + p * PIECE, PIECE), PIECE)
-            spread[at, 0 : 2 * LANES] = pltpu.matmul_pop(radius_acc[p])
-            spread[at, 2 * LANES :] = pltpu.matmul_pop(coupling_acc[p])[:, 0:LANES]
-            tgt_sum[at, :] = jnp.zeros((PIECE, 3 * LANES), F32)
-        return 0
-
-    lax.fori_loop(0, chunks, spread_prep, 0)
 
     zeros = jnp.zeros((WIDTH, BLOCK), BF16)
 
@@ -185,8 +167,38 @@
             src_table[pl.ds(pl.multiple_of(block * BLOCK, BLOCK), BLOCK), :] = jnp.transpose(stacked)
         return 0
 
-    fetch.wait()
+    fetches[0].wait()
     lax.fori_loop(0, parts, source_prep, 0)
+    fetches[1].wait()
+
+    feature = lax.broadcasted_iota(jnp.int32, (BLOCK, BLOCK), 0) - WIDTH
+    which = lax.broadcasted_iota(jnp.int32, (BLOCK, BLOCK), 1) // LANES
+    for unit in range(2):
+        axis = which + 2 * unit
+        pick = (feature == 5 + axis) | (feature == 16 + axis) | (feature == 25 + axis)
+        pltpu.matmul_push_rhs((pick & (axis < 3)).astype(F32).astype(BF16), 0, unit)
+    pltpu.matmul_acc_lhs(radius_acc[0], left_m[0:PIECE, :], load_staged_rhs=0)
+    pltpu.matmul_acc_lhs(coupling_acc[0], left_m[0:PIECE, :], load_staged_rhs=0)
+    pltpu.matmul_pop(radius_acc[0])
+    pltpu.matmul_pop(coupling_acc[0])
+
+    def spread_prep(i, _):
+        for p in range(count):
+            left = left_m[pl.ds(pl.multiple_of(i * CHUNK + p * PIECE, PIECE), PIECE), :]
+            pltpu.matmul_acc_lhs(radius_acc[p], left)
+            pltpu.matmul_acc_lhs(coupling_acc[p], left)
+        for p in range(count):
+            at = pl.ds(pl.multiple_of(i * CHUNK + p * PIECE, PIECE), PIECE)
+            spread[at, 0 : 2 * LANES] = pltpu.matmul_pop(radius_acc[p])
+            spread[at, 2 * LANES :] = pltpu.matmul_pop(coupling_acc[p])[:, 0:LANES]
+            tgt_sum[at, :] = jnp.zeros((PIECE, 3 * LANES), F32)
+        return 0
+
+    lax.fori_loop(0, chunks, spread_prep, 0)
+
+    for fetch in fetches[2:]:
+        fetch.wait()
+    first_target = (near_tgt[0] // tgt_count) * tgt_count
 
     steps = blocks * chunks
 
@@ -339,27 +351,28 @@
                 src_out[b, row : row + 1, :] = -far_sum - near[c : c + 1]
 
 
-def pair_sums(tgt_pos, tgt_area, tgt_cond, adjoint, cond_scale, near_tgt, near_src, near_coef, packs):
-    tgt_count = tgt_pos.shape[1]
+def pair_sums(held, left_m, near_tgt, near_src, near_coef, packs):
+    tgt_count = held.shape[0]
     pairs = near_coef.shape[0]
     parts, _, per = packs.shape
     total = parts * per
     blocks = total // BLOCK
-    vmem = pl.BlockSpec(memory_space=pltpu.VMEM)
-    smem = pl.BlockSpec(memory_space=pltpu.SMEM)
+    vmem, hbm = pl.BlockSpec(memory_space=pltpu.VMEM), pl.BlockSpec(memory_space=pl.ANY)
     return pl.pallas_call(
         pair_kernel,
         out_shape=[
             jax.ShapeDtypeStruct((3, tgt_count), F32),
             jax.ShapeDtypeStruct((parts, SUM_ROWS, LANES), F32),
         ],
-        in_specs=[smem, smem] + [vmem] * 8 + [pl.BlockSpec(memory_space=pl.ANY)],
+        in_specs=[hbm, hbm] + [vmem] * 3 + [hbm] * 3,
         out_specs=[vmem, vmem],
         scratch_shapes=[
+            pltpu.VMEM(held.shape, F32),
+            pltpu.VMEM(left_m.shape, BF16),
             pltpu.VMEM(packs.shape, F32),
-            pltpu.SemaphoreType.DMA,
-            pltpu.VMEM((tgt_count, LANES), F32),
-            pltpu.VMEM((tgt_count, 2 * LANES), BF16),
+            pltpu.SMEM((pairs,), jnp.int32),
+            pltpu.SMEM((pairs,), jnp.int32),
+            pltpu.SemaphoreType.DMA((5,)),
             pltpu.VMEM((blocks, 3, BLOCK, BLOCK), BF16),
             pltpu.VMEM((blocks, 8, BLOCK), F32),
             pltpu.VMEM((total, LANES), F32),
@@ -372,8 +385,7 @@
         ],
         compiler_params=pltpu.CompilerParams(vmem_limit_bytes=60 * 2**20),
     )(
-        near_tgt, near_src, tgt_pos, tgt_area[None, :], tgt_cond[None, :], adjoint, cond_scale[None, :],
-        near_tgt[None, :], near_src[None, :], near_coef[None, :], packs,
+        near_tgt, near_src, near_tgt[None, :], near_src[None, :], near_coef[None, :], held, left_m, packs,
     )
 
 
@@ -384,7 +396,17 @@
     pl.semaphore_wait(barrier, len(peers))
 
 
-def gather_kernel(density, pos, nrm, area, out, pack, send_sem, recv_sem, local_sem):
+def gather_kernel(
+    density, pos, nrm, area, tgt_pos_in, tgt_area, tgt_cond, adjoint_in, cond_scale,
+    out, held_out, left_out,
+    pack, tgt_pos, adjoint, held, left_m, send_sem, recv_sem, local_sem,
+):
+    reads = [
+        pltpu.make_async_copy(tgt_pos_in, tgt_pos, local_sem.at[1]),
+        pltpu.make_async_copy(adjoint_in, adjoint, local_sem.at[2]),
+    ]
+    for read in reads:
+        read.start()
     me, grp = lax.axis_index("blk"), lax.axis_index("grp")
     z, y_lo, core = me // 4, lax.rem(me // 2, 2), lax.rem(me, 2)
 
@@ -429,8 +451,25 @@
     send("up2", me, second, to_up)
     send("down2", me, first, to_down)
     send("c0", me, whole, to_mate)
-    mine = pltpu.make_async_copy(pack, out.at[me], local_sem)
+    mine = pltpu.make_async_copy(pack, out.at[me], local_sem.at[0])
     mine.start()
+
+    writes = []
+    turns = tgt_pos.shape[1] // CHUNK
+    stops = [turns * q // 4 for q in range(5)]
+
+    def prepare(q):
+        if q == 0:
+            for read in reads:
+                read.wait()
+        prepare_targets(stops[q], stops[q + 1], tgt_pos, tgt_area, tgt_cond, adjoint, cond_scale, held, left_m)
+        at = pl.ds(stops[q] * CHUNK, (stops[q + 1] - stops[q]) * CHUNK)
+        for i, (here, there) in enumerate(((held, held_out), (left_m, left_out))):
+            write = pltpu.make_async_copy(here.at[at], there.at[at], local_sem.at[3 + 2 * q + i])
+            write.start()
+            writes.append(write)
+
+    prepare(0)
     arrived("up1")
     send("on_up", down, first, to_up)
     send("y3a", down, first, to_beside)
@@ -443,39 +482,57 @@
     send("y1a", up, first, to_beside)
     send("c3", down, whole, to_mate)
     send("c1", up, whole, to_mate)
+    prepare(1)
     arrived("on_up")
     send("y2a", across, first, to_beside)
     arrived("on_down")
     send("y2b", across, second, to_around)
     send("c2", across, whole, to_mate)
+    prepare(2)
     for step in (0, 3, 1, 2):
         arrived("y%da" % step, "y%db" % step)
         send("cy%d" % step, block(z + step, 1 - y_lo, core), whole, to_mate)
+    prepare(3)
     for step in (0, 3, 1, 2):
         arrived("c%d" % step)
     for step in (0, 3, 1, 2):
         arrived("cy%d" % step)
     mine.wait()
+    for write in writes:
+        write.wait()
     for copy in copies.values():
         copy.wait_send()
 
 
-def gather_sources(density, pos, nrm, area, n):
+def gather_sources(density, pos, nrm, area, tgt_pos, tgt_area, tgt_cond, adjoint, cond_scale, n):
     vmem, hbm = pl.BlockSpec(memory_space=pltpu.VMEM), pl.BlockSpec(memory_space=pl.ANY)
     shape = (PACK, pos.shape[1])
+    tgt_count = tgt_pos.shape[1]
     return pl.pallas_call(
         gather_kernel,
-        out_shape=jax.ShapeDtypeStruct((n,) + shape, F32),
-        in_specs=[vmem] * 4,
-        out_specs=hbm,
+        out_shape=[
+            jax.ShapeDtypeStruct((n,) + shape, F32),
+            jax.ShapeDtypeStruct((tgt_count, LANES), F32),
+            jax.ShapeDtypeStruct((tgt_count, 2 * LANES), BF16),
+        ],
+        in_specs=[vmem] * 4 + [hbm, vmem, vmem, hbm, vmem],
+        out_specs=[hbm] * 3,
         scratch_shapes=[
             pltpu.VMEM(shape, F32),
+            pltpu.VMEM(tgt_pos.shape, F32),
+            pltpu.VMEM(adjoint.shape, F32),
+            pltpu.VMEM((tgt_count, LANES), F32),
+            pltpu.VMEM((tgt_count, 2 * LANES), BF16),
             pltpu.SemaphoreType.DMA((22,)),
             pltpu.SemaphoreType.DMA((22,)),
-            pltpu.SemaphoreType.DMA,
+            pltpu.SemaphoreType.DMA((11,)),
         ],
-        compiler_params=pltpu.CompilerParams(collective_id=0, has_side_effects=True),
-    )(density, pos, nrm, area[None, :])
+        compiler_params=pltpu.CompilerParams(
+            collective_id=0, has_side_effects=True, vmem_limit_bytes=60 * 2**20
+        ),
+    )(
+        density, pos, nrm, area[None, :], tgt_pos, tgt_area[None, :], tgt_cond[None, :], adjoint, cond_scale[None, :],
+    )
 
 
 def reduce_kernel(n, groups, sums, out, first, second, mine, send1, recv1, send2, recv2):
@@ -542,10 +599,10 @@
     tgt_pos, tgt_area, tgt_cond, adjoint, src_pos, src_nrm, src_area, density, cond_scale, near_tgt, near_src, near_coef
 ):
     n, groups = lax.axis_size("blk"), lax.axis_size("grp")
-    packs = gather_sources(density, src_pos, src_nrm, src_area, n)
-    tgt_grad, sums = pair_sums(
-        tgt_pos, tgt_area, tgt_cond, adjoint, cond_scale, near_tgt, near_src, near_coef, packs
-    )
+    packs, held, left_m = gather_sources(
+        density, src_pos, src_nrm, src_area, tgt_pos, tgt_area, tgt_cond, adjoint, cond_scale, n
+    )
+    tgt_grad, sums = pair_sums(held, left_m, near_tgt, near_src, near_coef, packs)
     return tgt_grad, reduce_sources(sums, n, groups)
 
 

time: 172 us -> 171 us (level)
  no operation moved by 1% of the time
where the time goes in v4:
time: 171 us
  Pallas kernels  169 us (99%)
    pallas_call x1, Pallas kernels, pair_sums(): pl.pallas_call(pair_kernel, out_shape=[jax.ShapeDtypeStruct((3, tgt_count...  133 us
    pallas_call x1, Pallas kernels, gather_sources(): pl.pallas_call(gather_kernel, out_shape=[jax.ShapeDtypeStruct((n,) + shap...  21.8 us
    pallas_call x1, Pallas kernels, reduce_sources(): pl.pallas_call(functools.partial(reduce_kernel, n, groups), out_shape=jax...  14.2 us

profile of v4, /device:TPU:1, one launch (start us, length us, event | category | flops | bytes accessed | tf_op | source)
XLA Modules:
  0.0 171.0 jit_solution(3417004484360269052)
XLA Ops:
  0.6 21.8 %shard_map.131 = (f32[16,72,512]{2,1,0:T(8,128)}, f32[4096,128]{1,0:T(8,128)}, bf16[4096,256]{1,0:T(8,128)(2,1)}) custom-call(f32[64,512]{1,0:T(8,128)} %density.1, f32[3,512]{1,0:T(4,128)} %pos.1, f32[3,512]{1,0:T(4,128)} %nrm.1, f32[1,512]{1,0:T(1,128)} %bitcast.12, f32[3,4096]{1,0:T(4,128)} %tgt_pos_in.1, f32[1,4096]{1,0:T(1,128)} %bitcast.9, ...), custom_call_target="tpu_custom_call" | custom-call | tf_op jit(solution)/shard_map/pallas_call | solution.py:511
  22.5 133.0 %shard_map.132 = (f32[3,4096]{1,0:T(4,128)}, f32[16,16,128]{2,1,0:T(8,128)}) custom-call(s32[4096]{0:T(1024)} %refs_0_.1, s32[4096]{0:T(1024)} %refs_1_.1, s32[1,4096]{1,0:T(1,128)} %bitcast.7, s32[1,4096]{1,0:T(1,128)} %bitcast.8, f32[1,4096]{1,0:T(1,128)} %bitcast.11, f32[4096,128]{1,0:T(8,128)} %get-tuple-element.7.refs_5_, ...), custom_call_target="tpu_custom_call" | custom-call | tf_op jit(solution)/shard_map/pallas_call | solution.py:361
  155.5 14.2 %shard_map.133 = f32[3,64]{1,0:T(4,128)} custom-call(f32[16,16,128]{2,1,0:T(8,128)} %get-tuple-element.11.sums), custom_call_target="tpu_custom_call" | custom-call | tf_op jit(solution)/shard_map/pallas_call | solution.py:580
  169.7 1.2 copy.15
